TPU v7x, 32 devices: a whole 2x2x4 slice. The times are simulated.
32 devices in a mesh: dp: 2 (over x), seq: 4 (over z), enc: 4 (over y, core).
Axes of the slice: x: 2, y: 2, z: 4, core: 2. Of those that a mesh axis runs over, the one named last changes fastest.
Arguments:
- queries: bfloat16 [8, 512, 512], P(('dp', 'enc'), 'seq'), may hold values from -12 to 12
- cotangent: bfloat16 [8, 512, 512], P(('dp', 'enc'), 'seq'), may hold values from -12 to 12
- key_pool: bfloat16 [2, 4, 8, 128, 512], P('dp', 'seq', None, None, 'enc'), may hold values from -12 to 12
- value_pool: bfloat16 [2, 4, 8, 128, 512], P('dp', 'seq', None, None, 'enc'), may hold values from -6 to 6
- counts: int32 [8, 8], P('dp', 'seq'), may hold values from 0 to 4
- neighbour_ids: int32 [8, 8, 4], P('dp', 'seq'), may hold values from 0 to 7, all different within a row
- rel_bias: float32 [4, 191], P('enc'), may hold values from -3 to 3
Outputs:
- context: bfloat16 [8, 512, 512], P(('dp', 'enc'), 'seq')
- query_grad: bfloat16 [8, 512, 512], P(('dp', 'enc'), 'seq')
- key_grad: bfloat16 [2, 4, 8, 128, 512], P('dp', 'seq', None, None, 'enc')
- value_grad: bfloat16 [2, 4, 8, 128, 512], P('dp', 'seq', None, None, 'enc')
- bias_grad: float32 [4, 191], P('enc')
Inputs may be any that keep to these rules, and one draw needn't show every extreme that they name: Only the first counts[c] ids of a block are used. `neighbour_ids`: the 4 ids of one block are distinct.
All inputs are finite; a program needn't handle non-finite values.
Results may differ from a plain program's by a relative error of at most 0.0085.
Values may be sent and summed in bfloat16 or wider, within the bound.
A program may use at most 64 MiB of HBM per device.

v0:
```python
import math

import jax
import jax.numpy as jnp
from jax import lax
from jax.sharding import PartitionSpec as P

HEAD_DIM = 128
BLOCK_LEN = 64
PASSAGE = 128


NEG_FILL = -1e30


def bias_rows(bias_table):
    heads_here, table_width = bias_table.shape
    padded = jnp.pad(bias_table, ((0, 0), (0, 1)))
    tiled_rows = jnp.broadcast_to(padded[:, None, :], (heads_here, BLOCK_LEN, table_width + 1))
    tiled_rows = tiled_rows.reshape(heads_here, BLOCK_LEN * (table_width + 1))[
        :, : BLOCK_LEN * table_width
    ]
    tiled_rows = tiled_rows.reshape(heads_here, BLOCK_LEN, table_width)
    return tiled_rows[:, :, BLOCK_LEN - 1 : BLOCK_LEN - 1 + PASSAGE]


def fold_bias(totals, table_width):
    heads_here = totals.shape[0]
    padded = jnp.pad(totals, ((0, 0), (0, 0), (BLOCK_LEN - 1, 0)))
    flat_rows = padded.reshape(heads_here, BLOCK_LEN * table_width)
    flat_rows = jnp.pad(flat_rows, ((0, 0), (0, BLOCK_LEN)))
    return flat_rows.reshape(heads_here, BLOCK_LEN, table_width + 1).sum(axis=1)[:, :table_width]


def forward_pass(query_heads, id_table, count_table, pool_keys, pool_values, row_bias):
    score_scale = 1.0 / math.sqrt(HEAD_DIM)
    block_total = query_heads.shape[0]
    batch_blocks = 8
    batch_count = block_total // batch_blocks

    def forward_one_batch(pieces):
        query_block, id_block, count_block = pieces
        keys_sel = pool_keys[id_block]
        values_sel = pool_values[id_block]
        scores = (
            jnp.einsum(
                "cqhd,cjthd->chqjt", query_block, keys_sel, preferred_element_type=jnp.float32
            )
            * score_scale
        )
        scores = scores + row_bias[None, :, :, None, :]
        slot_index = jnp.arange(id_block.shape[1])
        usable = (slot_index[None, :] < count_block[:, None])[:, None, None, :, None]
        row_top = jnp.max(jnp.where(usable, scores, NEG_FILL), axis=(3, 4), keepdims=True)
        raised = jnp.where(usable, jnp.exp(scores - row_top), 0.0)
        no_keys = (count_block == 0).astype(jnp.float32)[:, None, None, None, None]
        weights = raised / (jnp.sum(raised, axis=(3, 4), keepdims=True) + no_keys)
        context_block = jnp.einsum(
            "chqjt,cjthd->cqhd",
            weights.astype(jnp.bfloat16),
            values_sel,
            preferred_element_type=jnp.float32,
        )
        return (context_block.astype(jnp.bfloat16), weights)

    context_blocks, weight_blocks = lax.map(
        forward_one_batch,
        (
            query_heads.reshape((batch_count, batch_blocks) + query_heads.shape[1:]),
            id_table.reshape(batch_count, batch_blocks, id_table.shape[1]),
            count_table.reshape(batch_count, batch_blocks),
        ),
    )
    return (context_blocks.reshape(query_heads.shape), weight_blocks)


def backward_pass(query_heads, grad_heads, weight_blocks, id_table, pool_keys, pool_values):
    score_scale = 1.0 / math.sqrt(HEAD_DIM)
    batch_count, batch_blocks = (weight_blocks.shape[0], weight_blocks.shape[1])
    pool_size = pool_keys.shape[0]
    heads_here = pool_keys.shape[2]

    def backward_one_batch(running, pieces):
        key_total, value_total, bias_total = running
        query_block, grad_block, weights, id_block = pieces
        keys_sel = pool_keys[id_block]
        values_sel = pool_values[id_block]
        grad_weights = jnp.einsum(
            "cqhd,cjthd->chqjt", grad_block, values_sel, preferred_element_type=jnp.float32
        )
        row_delta = jnp.sum(weights * grad_weights, axis=(3, 4), keepdims=True)
        grad_scores = weights * (grad_weights - row_delta)
        scores_low = grad_scores.astype(jnp.bfloat16)
        weights_low = weights.astype(jnp.bfloat16)
        query_block_grad = score_scale * jnp.einsum(
            "chqjt,cjthd->cqhd", scores_low, keys_sel, preferred_element_type=jnp.float32
        )
        key_slots = jnp.einsum(
            "chqjt,cqhd->cjthd", scores_low, query_block, preferred_element_type=jnp.float32
        )
        value_slots = jnp.einsum(
            "chqjt,cqhd->cjthd", weights_low, grad_block, preferred_element_type=jnp.float32
        )
        flat_ids = id_block.reshape(-1)
        key_total = key_total.at[flat_ids].add(key_slots.reshape((-1,) + key_slots.shape[2:]))
        value_total = value_total.at[flat_ids].add(
            value_slots.reshape((-1,) + value_slots.shape[2:])
        )
        bias_total = bias_total + jnp.sum(grad_scores, axis=(0, 3))
        return ((key_total, value_total, bias_total), query_block_grad.astype(jnp.bfloat16))

    pool_zeros = jnp.zeros((pool_size, PASSAGE, heads_here, HEAD_DIM), jnp.float32)
    bias_zeros = jnp.zeros((heads_here, BLOCK_LEN, PASSAGE), jnp.float32)
    running, query_grads = lax.scan(
        backward_one_batch,
        (pool_zeros, pool_zeros, bias_zeros),
        (
            query_heads.reshape((batch_count, batch_blocks) + query_heads.shape[1:]),
            grad_heads.reshape((batch_count, batch_blocks) + grad_heads.shape[1:]),
            weight_blocks,
            id_table.reshape(batch_count, batch_blocks, id_table.shape[1]),
        ),
    )
    key_total, value_total, bias_total = running
    return (
        query_grads.reshape(query_heads.shape),
        score_scale * key_total,
        value_total,
        bias_total,
    )


def local(queries, cotangent, key_pool, value_pool, counts, neighbour_ids, rel_bias):
    token_rows = queries.shape[1]
    full_width = queries.shape[2]
    blocks_here = token_rows // BLOCK_LEN
    head_width = key_pool.shape[-1]
    heads_here = head_width // HEAD_DIM
    pool_size = key_pool.shape[2]
    pool_keys = key_pool.reshape(pool_size, PASSAGE, heads_here, HEAD_DIM)
    pool_values = value_pool.reshape(pool_size, PASSAGE, heads_here, HEAD_DIM)
    id_table = neighbour_ids.reshape(-1, neighbour_ids.shape[-1])
    count_table = counts.reshape(-1)
    row_bias = bias_rows(rel_bias)
    query_rows = queries.reshape(blocks_here, BLOCK_LEN, full_width)
    grad_rows = cotangent.reshape(blocks_here, BLOCK_LEN, full_width)

    def to_heads(moved_rows):
        return moved_rows.reshape(moved_rows.shape[0], BLOCK_LEN, heads_here, HEAD_DIM)

    def to_rows(head_rows):
        return head_rows.reshape(head_rows.shape[0], BLOCK_LEN, head_width)

    query_heads = to_heads(
        lax.all_to_all(query_rows, "enc", split_axis=2, concat_axis=0, tiled=True)
    )
    context_heads, weight_blocks = forward_pass(
        query_heads, id_table, count_table, pool_keys, pool_values, row_bias
    )
    context_rows = lax.all_to_all(
        to_rows(context_heads), "enc", split_axis=0, concat_axis=2, tiled=True
    )
    grad_heads = to_heads(lax.all_to_all(grad_rows, "enc", split_axis=2, concat_axis=0, tiled=True))
    query_part, key_total, value_total, bias_total = backward_pass(
        query_heads, grad_heads, weight_blocks, id_table, pool_keys, pool_values
    )
    query_back = lax.all_to_all(to_rows(query_part), "enc", split_axis=0, concat_axis=2, tiled=True)
    bias_grad = lax.psum(fold_bias(bias_total, rel_bias.shape[1]), ("dp", "seq"))
    return (
        context_rows.reshape(queries.shape),
        query_back.reshape(queries.shape),
        key_total.astype(jnp.bfloat16).reshape(key_pool.shape),
        value_total.astype(jnp.bfloat16).reshape(value_pool.shape),
        bias_grad,
    )


def solution(mesh):
    in_specs = (
        P(("dp", "enc"), "seq", None),
        P(("dp", "enc"), "seq", None),
        P("dp", "seq", None, None, "enc"),
        P("dp", "seq", None, None, "enc"),
        P("dp", "seq"),
        P("dp", "seq", None),
        P("enc", None),
    )
    out_specs = (
        P(("dp", "enc"), "seq", None),
        P(("dp", "enc"), "seq", None),
        P("dp", "seq", None, None, "enc"),
        P("dp", "seq", None, None, "enc"),
        P("enc", None),
    )
    return jax.shard_map(local, mesh=mesh, in_specs=in_specs, out_specs=out_specs, check_vma=False)
```

profile of v0, /device:TPU:0, one launch (start us, length us, event | category | flops | bytes accessed | tf_op | source)
XLA Modules:
  0.0 73.0 jit_solution(3560335956245950353)
XLA Ops:
  0.6 1.1 %copy.39 = bf16[2,64,512]{1,0,2:T(2,128)(2,1)S(1)} copy(bf16[2,64,512]{2,1,0:T(8,128)(2,1)} %bitcast.121) | data formatting | bytes 262144 | tf_op jit(solution)/shard_map/reshape | solution.py:145
  1.8 0.9 %reshape.345 = bf16[4,2,8192]{2,1,0:T(2,128)(2,1)} reshape(bf16[512,2,64]{2,1,0:T(2,128)(2,1)S(1)} %bitcast.113) | data formatting | bytes 262144
  2.7 4.2 %all-to-all-start = ((bf16[4,2,8192]{2,1,0:T(2,128)(2,1)}), bf16[4,2,8192]{2,1,0:T(2,128)(2,1)S(1)}, u32[]{:S(2)}, u32[]{:S(2)}) async-start(bf16[4,2,8192]{2,1,0:T(2,128)(2,1)} %reshape.345), calls=%async_computation | async-start | bytes 262144 | tf_op jit(solution)/shard_map/all_to_all | solution.py:155
  6.9 0.8 %copy.38 = s32[4,2]{1,0:T(4,128)S(1)} copy(s32[4,2]{0,1:T(2,128)} %param.11) | data formatting | bytes 64 | tf_op args[4]
  7.7 0.1 lt.57
  7.8 0.1 iota_compare_fusion
  7.8 0.8 %reshape.266 = s32[32,1]{0,1:T(1,128)S(1)} reshape(s32[4,2,4]{2,1,0:T(2,128)} %param.12) | data formatting | bytes 256 | tf_op jit(solution)/shard_map/while/body/eval_jaxpr/reshape | solution.py:104
  8.6 0.7 compare_select_fusion
  9.3 0.7 pad.12
  10.0 0.1 broadcast_in_dim.74
  10.1 0.1 slice_reduce_fusion
  10.2 0.2 reshape.261
  10.4 0.7 slice_bitcast_fusion
  11.1 0.5 fusion.15
  11.7 0.1 reshape.277
  11.7 1.1 %copy.43 = bf16[2,64,512]{1,0,2:T(2,128)(2,1)S(1)} copy(bf16[2,64,512]{2,1,0:T(8,128)(2,1)} %bitcast.122) | data formatting | bytes 262144 | tf_op jit(solution)/shard_map/reshape | solution.py:146
  12.8 0.9 %reshape.347 = bf16[4,2,8192]{2,1,0:T(2,128)(2,1)} reshape(bf16[512,2,64]{2,1,0:T(2,128)(2,1)S(1)} %bitcast.114) | data formatting | bytes 262144
  13.7 3.3 %all-to-all-start.2 = ((bf16[4,2,8192]{2,1,0:T(2,128)(2,1)}), bf16[4,2,8192]{2,1,0:T(2,128)(2,1)S(1)}, u32[]{:S(2)}, u32[]{:S(2)}) async-start(bf16[4,2,8192]{2,1,0:T(2,128)(2,1)} %reshape.347), calls=%async_computation.2 | async-start | bytes 262144 | tf_op jit(solution)/shard_map/all_to_all | solution.py:163
  17.1 0.7 %gather_fusion = bf16[32,128,128]{2,1,0:T(8,128)(2,1)S(1)} fusion(bf16[8,128,128]{2,1,0:T(8,128)(2,1)S(1)} %bitcast.103, s32[1024]{0:T(1024)S(1)} %pad_clamp_fusion), kind=kCustom, calls=%fused_computation | custom fusion | bytes 2097280 | tf_op jit(solution)/shard_map/while/body/eval_jaxpr/gather | solution.py:44
  17.8 0.7 %gather_fusion.1 = bf16[32,128,128]{2,1,0:T(8,128)(2,1)S(1)} fusion(bf16[8,128,128]{2,1,0:T(8,128)(2,1)S(1)} %bitcast.107, s32[1024]{0:T(1024)S(1)} %pad_clamp_fusion), kind=kCustom, calls=%fused_computation.1 | custom fusion | bytes 2097280 | tf_op jit(solution)/shard_map/while/body/eval_jaxpr/gather | solution.py:43
  18.6 0.2 reshape.346
  18.8 0.2 copy.51
  19.0 2.7 %all-to-all-done.2 = bf16[4,2,8192]{2,1,0:T(2,128)(2,1)S(1)} async-done(((bf16[4,2,8192]{2,1,0:T(2,128)(2,1)}), bf16[4,2,8192]{2,1,0:T(2,128)(2,1)S(1)}, u32[]{:S(2)}, u32[]{:S(2)}) %all-to-all-start.2) | async-done | bytes 131104 | tf_op jit(solution)/shard_map/all_to_all | solution.py:163
  21.7 0.2 reshape.348
  21.9 0.2 copy.52
  22.1 1.3 %select_reduce_fusion = (f32[8,64]{1,0:T(8,128)S(1)}, f32[8,64,4,128]{3,1,2,0:T(8,128)S(1)}) fusion(pred[8,4]{1,0:T(8,128)(4,1)S(1)} %iota_compare_fusion, f32[64,128]{1,0:T(8,128)} %slice_bitcast_fusion, bf16[8,4,128,128]{3,2,1,0:T(8,128)(2,1)S(1)} %bitcast.104, bf16[8,64,128,1]{2,1,3,0:T(8,128)(2,1)S(1)} %bitcast.109), kind=kOutput, calls=%fused_computation.18 | convolution fusion | flops 68156928 | bytes 2263072 | tf_op jit(solution)/shard_map/while/body/eval_jaxpr/cqhd,cjthd->chqjt/dot_general | solution.py:46
  23.4 0.4 fusion.8
  23.8 0.1 broadcast_add_fusion
  23.9 1.1 %fusion.6 = bf16[8,64,128]{2,1,0:T(8,128)(2,1)} fusion(bf16[8,4,128,128]{3,2,1,0:T(8,128)(2,1)S(1)} %bitcast.115, f32[8,64,4,128]{3,1,2,0:T(8,128)S(1)} %get-tuple-element.46, f32[8,64]{1,0:T(8,128)S(1)} %broadcast_add_fusion, f32[8,64]{1,0:T(8,128)S(1)} %get-tuple-element.45, pred[8,4]{1,0:T(8,128)(4,1)S(1)} %iota_compare_fusion), kind=kOutput, calls=%fused_computation.14 | convolution fusion | flops 68222976 | bytes 2232352 | tf_op jit(solution)/shard_map/while/body/eval_jaxpr/chqjt,cjthd->cqhd/dot_general | solution.py:58
  25.0 1.5 %multiply_reduce_fusion = (f32[8,64]{1,0:T(8,128)S(1)}, f32[8,64,4,128]{3,1,2,0:T(8,128)}) fusion(f32[8,64]{1,0:T(8,128)S(1)} %broadcast_add_fusion, f32[8,64,4,128]{3,1,2,0:T(8,128)S(1)} %get-tuple-element.46, f32[8,64]{1,0:T(8,128)S(1)} %get-tuple-element.45, pred[8,4]{1,0:T(8,128)(4,1)S(1)} %iota_compare_fusion, ...), kind=kOutput, calls=%fused_computation.16 | convolution fusion | flops 68419072 | bytes 3282976 | tf_op jit(solution)/shard_map/while/body/eval_jaxpr/cqhd,cjthd->chqjt/dot_general | solution.py:88
  26.5 2.3 %fusion.12 = f32[8,4,128,128]{3,2,1,0:T(8,128)} fusion(bf16[8,64,128,1]{2,1,3,0:T(8,128)(2,1)S(1)} %bitcast.124, f32[8,64,4,128]{3,1,2,0:T(8,128)S(1)} %get-tuple-element.46, f32[8,64]{1,0:T(8,128)S(1)} %broadcast_add_fusion, f32[8,64]{1,0:T(8,128)S(1)} %get-tuple-element.45, pred[8,4]{1,0:T(8,128)(4,1)S(1)} %iota_compare_fusion), kind=kOutput, calls=%fused_computation.26 | convolution fusion | flops 68157440 | bytes 3280928 | tf_op jit(solution)/shard_map/while/body/eval_jaxpr/chqjt,cqhd->cjthd/dot_general | solution.py:101
  28.8 3.9 %all-to-all-start.1 = ((bf16[8,64,128]{2,1,0:T(8,128)(2,1)}), bf16[8,64,128]{2,1,0:T(8,128)(2,1)}, u32[]{:S(2)}, u32[]{:S(2)}) async-start(bf16[8,64,128]{2,1,0:T(8,128)(2,1)} %fusion.6), calls=%async_computation.1 | async-start | bytes 262144 | tf_op jit(solution)/shard_map/all_to_all | solution.py:160
  32.7 1.1 %fusion.9 = (f32[64,128]{1,0:T(8,128)}, bf16[8,64,4,128]{3,1,2,0:T(8,128)(2,1)S(1)}) fusion(f32[8,64,4,128]{3,1,2,0:T(8,128)S(1)} %copy-done.2, f32[8,64]{1,0:T(8,128)S(1)} %get-tuple-element.58, f32[8,64]{1,0:T(8,128)S(1)} %broadcast_add_fusion, f32[8,64,4,128]{3,1,2,0:T(8,128)S(1)} %get-tuple-element.46, f32[8,64]{1,0:T(8,128)S(1)} %get-tuple-element.45, ...), kind=kLoop, calls=%fused_computation.22 | loop fusion | flops 1826816 | bytes 2660384 | tf_op jit(solution)/shard_map/while/body/eval_jaxpr/reduce_sum | solution.py:109
  33.8 0.5 fusion.18
  34.4 1.0 %fusion.5 = bf16[8,64,128]{2,1,0:T(8,128)(2,1)} fusion(bf16[8,64,4,128]{3,1,2,0:T(8,128)(2,1)S(1)} %get-tuple-element.44, bf16[8,4,128,128]{3,2,1,0:T(8,128)(2,1)S(1)} %bitcast.105), kind=kOutput, calls=%fused_computation.13 | convolution fusion | flops 67239936 | bytes 1703936 | tf_op jit(solution)/shard_map/while/body/eval_jaxpr/chqjt,cjthd->cqhd/dot_general | solution.py:95
  35.4 2.7 %scatter_fusion = f32[8,128,128]{2,1,0:T(8,128)S(1)} fusion(f32[8,128,128]{2,1,0:T(8,128)S(1)} %broadcast.128.clone, s32[32]{0:T(128)S(1)} %copy-done.4, f32[32,128,128]{2,1,0:T(8,128)S(1)} %bitcast.106), kind=kCustom, calls=%fused_computation.2 | custom fusion | flops 524288 | bytes 6291584 | tf_op jit(solution)/shard_map/while/body/eval_jaxpr/scatter-add | solution.py:105
  38.1 4.7 %scatter_fusion.1 = f32[8,128,128]{2,1,0:T(8,128)S(1)} fusion(f32[8,128,128]{2,1,0:T(8,128)S(1)} %broadcast.128.clone.1, s32[32]{0:T(128)S(1)} %copy-done.4, f32[32,128,128]{2,1,0:T(8,128)} %bitcast.108), kind=kCustom, calls=%fused_computation.3 | custom fusion | flops 524288 | bytes 6291584 | tf_op jit(solution)/shard_map/while/body/eval_jaxpr/scatter-add | solution.py:106
  42.8 3.3 %all-to-all-start.3 = ((bf16[8,64,128]{2,1,0:T(8,128)(2,1)}), bf16[8,64,128]{2,1,0:T(8,128)(2,1)S(1)}, u32[]{:S(2)}, u32[]{:S(2)}) async-start(bf16[8,64,128]{2,1,0:T(8,128)(2,1)} %fusion.5), calls=%async_computation.3 | async-start | bytes 262144 | tf_op jit(solution)/shard_map/all_to_all | solution.py:167
  46.1 0.9 %fusion.11 = (bf16[1,1,8,128,128]{4,3,2,1,0:T(8,128)(2,1)}, bf16[1,1,8,128,128]{4,3,2,1,0:T(8,128)(2,1)}) fusion(f32[8,128,128]{2,1,0:T(8,128)S(1)} %scatter_fusion, f32[8,128,128]{2,1,0:T(8,128)S(1)} %scatter_fusion.1), kind=kLoop, calls=%fused_computation.24 | loop fusion | flops 393216 | bytes 1572864 | tf_op jit(solution)/shard_map/reshape | solution.py:172
  47.0 0.1 pad.13
  47.1 0.3 reshape.271
  47.4 0.1 pad_reduce_fusion
  47.5 0.1 reshape.272
  47.6 22.8 %psum.7 = f32[1,191]{1,0:T(1,128)} all-reduce(f32[1,191]{1,0:T(1,128)S(1)} %bitcast.126), channel_id=1, replica_groups=mesh['dp'=2,'seq'=4,'enc'=4] {'dp','seq'}, use_global_device_ids=true, to_apply=%region_7.8 | all-reduce | flops 191 | bytes 1528 | tf_op jit(solution)/shard_map/psum | solution.py:168
  70.4 1.0 %copy.42 = bf16[2,64,4,128]{3,2,1,0:T(4,128)(2,1)S(1)} copy(bf16[2,64,4,128]{3,1,0,2:T(8,128)(2,1)} %bitcast.20) | data formatting | bytes 262144 | tf_op jit(solution)/shard_map/all_to_all | solution.py:160
  71.5 0.7 reshape.262
  72.2 0.1 copy.46
  72.3 0.7 reshape.265
  (21 shorter events, 0.2 us)
Async XLA Ops:
  0.6 16.4 %copy-start = (bf16[1,1,8,128,128]{4,3,2,1,0:T(8,128)(2,1)S(1)}, bf16[1,1,8,128,128]{4,3,2,1,0:T(8,128)(2,1)}, u32[]{:S(2)}) copy-start(bf16[1,1,8,128,128]{4,3,2,1,0:T(8,128)(2,1)} %param.10) | copy-start | bytes 786436
  1.8 16.1 %copy-start.1 = (bf16[1,1,8,128,128]{4,3,2,1,0:T(8,128)(2,1)S(1)}, bf16[1,1,8,128,128]{4,3,2,1,0:T(8,128)(2,1)}, u32[]{:S(2)}) copy-start(bf16[1,1,8,128,128]{4,3,2,1,0:T(8,128)(2,1)} %param.9) | copy-start | bytes 786436
  2.7 11.0 %all-to-all-start = ((bf16[4,2,8192]{2,1,0:T(2,128)(2,1)}), bf16[4,2,8192]{2,1,0:T(2,128)(2,1)S(1)}, u32[]{:S(2)}, u32[]{:S(2)}) async-start(bf16[4,2,8192]{2,1,0:T(2,128)(2,1)} %reshape.345), calls=%async_computation | async-start | bytes 262144 | tf_op jit(solution)/shard_map/all_to_all | solution.py:155
  13.7 8.0 %all-to-all-start.2 = ((bf16[4,2,8192]{2,1,0:T(2,128)(2,1)}), bf16[4,2,8192]{2,1,0:T(2,128)(2,1)S(1)}, u32[]{:S(2)}, u32[]{:S(2)}) async-start(bf16[4,2,8192]{2,1,0:T(2,128)(2,1)} %reshape.347), calls=%async_computation.2 | async-start | bytes 262144 | tf_op jit(solution)/shard_map/all_to_all | solution.py:163
  26.5 6.3 %copy-start.2 = (f32[8,64,4,128]{3,1,2,0:T(8,128)S(1)}, f32[8,64,4,128]{3,1,2,0:T(8,128)}, u32[]{:S(2)}) copy-start(f32[8,64,4,128]{3,1,2,0:T(8,128)} %get-tuple-element.59) | copy-start | bytes 3145732
  28.8 14.0 %all-to-all-start.1 = ((bf16[8,64,128]{2,1,0:T(8,128)(2,1)}), bf16[8,64,128]{2,1,0:T(8,128)(2,1)}, u32[]{:S(2)}, u32[]{:S(2)}) async-start(bf16[8,64,128]{2,1,0:T(8,128)(2,1)} %fusion.6), calls=%async_computation.1 | async-start | bytes 262144 | tf_op jit(solution)/shard_map/all_to_all | solution.py:160
  33.8 1.5 %copy-start.4 = (s32[32]{0:T(128)S(1)}, s32[32]{0:T(128)}, u32[]{:S(2)}) copy-start(s32[32]{0:T(128)} %fusion.15) | copy-start | bytes 388
  38.1 8.9 %copy-start.3 = (f32[64,128]{1,0:T(8,128)S(1)}, f32[64,128]{1,0:T(8,128)}, u32[]{:S(2)}) copy-start(f32[64,128]{1,0:T(8,128)} %get-tuple-element.43) | copy-start | bytes 98308
  42.8 29.4 %all-to-all-start.3 = ((bf16[8,64,128]{2,1,0:T(8,128)(2,1)}), bf16[8,64,128]{2,1,0:T(8,128)(2,1)S(1)}, u32[]{:S(2)}, u32[]{:S(2)}) async-start(bf16[8,64,128]{2,1,0:T(8,128)(2,1)} %fusion.5), calls=%async_computation.3 | async-start | bytes 262144 | tf_op jit(solution)/shard_map/all_to_all | solution.py:167
where the time goes:
time: 73.8 us; the launch traced here: 73 us
  blocking collectives  22.8 us (31%)
  starting transfers between devices  14.8 us (20%)
  local copies, waits for them, and re-layouts  13 us (18%)
  other arithmetic  11.1 us (15%)
  matrix products  7.7 us (10%)
  waiting for transfers between devices  2.67 us (4%)
  between operations  0.89 us (1%)
    psum x1, blocking collectives, local(): lax.psum(fold_bias(bias_total, rel_bias.shape[1]), ('dp', 'seq'))  22.8 us
    scatter-add x1, other arithmetic, backward_one_batch(): value_total.at[flat_ids]  4.66 us
    all_to_all x1, starting transfers between devices, local(): lax.all_to_all(query_rows, 'enc', split_axis=2, concat_axis=0, tiled=True)  4.24 us
    all_to_all x1, starting transfers between devices, local(): lax.all_to_all(to_rows(context_heads), 'enc', split_axis=0, concat_axis=2...  3.94 us
    all_to_all x1, starting transfers between devices, local(): lax.all_to_all(to_rows(query_part), 'enc', split_axis=0, concat_axis=2, t...  3.33 us
    all_to_all x1, starting transfers between devices, local(): lax.all_to_all(grad_rows, 'enc', split_axis=2, concat_axis=0, tiled=True)  3.33 us
    unnamed x15, local copies, waits for them, and re-layouts  3.02 us
    scatter-add x1, other arithmetic, backward_one_batch(): key_total.at[flat_ids].add(key_slots.reshape((-1,) + key_slots.shape[2:]))  2.66 us
  transfers between devices with their start and end apart: 4, of which 1 were waited for; matrix products, arithmetic and copies ran while one was open for 30% of the time, Pallas kernels for 0%

commit v1 on v0

v1 whole, which is shorter than its diff:
```python
import functools
import math

import jax
import jax.numpy as jnp
from jax import lax
from jax.experimental import pallas as pl
from jax.experimental.pallas import tpu as pltpu
from jax.sharding import PartitionSpec as P

HEAD_DIM = 128
BLOCK_LEN = 64
PASSAGE = 128
ROWS = 128
WIDE = 256

NEG_FILL = -1e30
SCALE = 1.0 / math.sqrt(HEAD_DIM)
LOG2E = math.log2(math.e)
F32 = jnp.float32
BF16 = jnp.bfloat16
MESH = pl.DeviceIdType.MESH


def each(low, high, body):
    if high - low <= 8:
        for step in range(low, high):
            body(step)
    else:

        def one(step, carry):
            body(step)
            return carry

        lax.fori_loop(low, high, one, 0)


def span(index):
    if isinstance(index, int):
        return pl.ds(index * ROWS, ROWS)
    return pl.ds(pl.multiple_of(index * ROWS, ROWS), ROWS)


def dot(left, right, left_dim, right_dim):
    return lax.dot_general(
        left, right, (((left_dim,), (right_dim,)), ((), ())), preferred_element_type=F32
    )


def spread_bias(line):
    rows = jnp.broadcast_to(line * LOG2E, (8, WIDE))
    sub = lax.broadcasted_iota(jnp.int32, (8, WIDE), 0)
    rows = pltpu.roll(rows, WIDE - (BLOCK_LEN - 1), 1)
    for bit in (1, 2, 4):
        rows = jnp.where((sub & bit) != 0, pltpu.roll(rows, bit, 1), rows)
    groups = [rows] + [pltpu.roll(rows, 8 * k, 1) for k in range(1, BLOCK_LEN // 8)]
    block = jnp.concatenate([group[:, :PASSAGE] for group in groups], axis=0)
    return jnp.concatenate([block, block], axis=0).T


def fold_bias(total):
    turned = total.T
    block = turned[:BLOCK_LEN] + turned[BLOCK_LEN:]
    block = jnp.concatenate([block, jnp.zeros((BLOCK_LEN, WIDE - PASSAGE), F32)], axis=1)
    for half in (32, 16, 8):
        block = pltpu.roll(block[:half], half, 1) + block[half : 2 * half]
    sub = lax.broadcasted_iota(jnp.int32, (8, WIDE), 0)
    for bit in (4, 2, 1):
        block = jnp.where((sub & bit) == 0, pltpu.roll(block, bit, 1), block)
    return jnp.sum(block, axis=0, keepdims=True)


def kernel(
    n_dp, n_seq, n_enc, pool, slots,
    q_hbm, g_hbm, k_hbm, v_hbm, count_hbm, id_hbm, bias_hbm,
    context_out, query_out, key_out, value_out, bias_out,
    q_buf, g_buf, k_buf, v_buf, k_turn, v_turn, counts, ids, line, wide_line, bias_map,
    s_buf, d_buf, w_all, ds_all, bias_sum, c_buf, dq_buf, dk_buf, dv_buf, parts, bias_row,
    load_sem, own_sem, store_sem,
    q_send, q_recv, g_send, g_recv, c_send, c_recv, dq_send, dq_recv, b_send, b_recv,
):
    dp, seq, enc = lax.axis_index("dp"), lax.axis_index("seq"), lax.axis_index("enc")
    total = n_dp * n_seq
    flat = dp * n_seq + seq
    table = line.shape[1]

    def to_peer(step):
        return lax.rem(enc + step, n_enc)

    def from_peer(step):
        return lax.rem(enc + (n_enc - step), n_enc)

    def group_at(place):
        return (place // n_seq, lax.rem(place, n_seq), enc)

    def other(step):
        return lax.rem(flat + step, total)

    barrier = pltpu.get_barrier_semaphore()

    def greet(step):
        pl.semaphore_signal(barrier, inc=1, device_id=(dp, seq, to_peer(step)), device_id_type=MESH)

    def greet_group(step):
        pl.semaphore_signal(barrier, inc=1, device_id=group_at(other(step)), device_id_type=MESH)

    each(1, n_enc, greet)
    each(1, total, greet_group)

    loads = [
        (bias_hbm, line),
        (count_hbm, counts),
        (id_hbm, ids),
        (k_hbm, k_buf),
        (q_hbm.at[0, :, span(enc)], q_buf.at[span(0)]),
        (v_hbm, v_buf),
        (g_hbm.at[0, :, span(enc)], g_buf.at[span(0)]),
    ]
    loads = [pltpu.make_async_copy(a, b, load_sem.at[i]) for i, (a, b) in enumerate(loads)]
    for load in loads:
        load.start()
    for load in loads[:3]:
        load.wait()

    wide_line[...] = jnp.zeros_like(wide_line)
    wide_line[:, 0:table] = line[...]
    bias_map[...] = spread_bias(wide_line[...])
    bias_sum[...] = jnp.zeros_like(bias_sum)

    pl.semaphore_wait(barrier, n_enc - 1 + total - 1)

    def q_copy(step):
        return pltpu.make_async_remote_copy(
            q_hbm.at[0, :, span(to_peer(step))], q_buf.at[span(step)],
            q_send.at[step], q_recv.at[step], (dp, seq, to_peer(step)), MESH,
        )

    def g_copy(step):
        return pltpu.make_async_remote_copy(
            g_hbm.at[0, :, span(to_peer(step))], g_buf.at[span(step)],
            g_send.at[step], g_recv.at[step], (dp, seq, to_peer(step)), MESH,
        )

    def c_copy(step, column):
        return pltpu.make_async_remote_copy(
            c_buf.at[span(step)], context_out.at[0, :, span(column)],
            c_send.at[step], c_recv.at[step], (dp, seq, from_peer(step)), MESH,
        )

    def dq_copy(step, column):
        return pltpu.make_async_remote_copy(
            dq_buf.at[span(step)], query_out.at[0, :, span(column)],
            dq_send.at[step], dq_recv.at[step], (dp, seq, from_peer(step)), MESH,
        )

    def b_copy(step, place):
        return pltpu.make_async_remote_copy(
            bias_row, parts.at[place],
            b_send.at[step], b_recv.at[step], group_at(other(step)), MESH,
        )

    def send_inputs(step):
        q_copy(step).start()
        g_copy(step).start()

    each(1, n_enc, send_inputs)

    for load in loads[3:]:
        load.wait()
    for p in range(pool):
        k_turn[:, p * PASSAGE : (p + 1) * PASSAGE] = k_buf[p * PASSAGE : (p + 1) * PASSAGE, :].T
        v_turn[:, p * PASSAGE : (p + 1) * PASSAGE] = v_buf[p * PASSAGE : (p + 1) * PASSAGE, :].T

    def weigh(step):
        source = from_peer(step)
        s_buf[...] = dot(k_buf[...], q_buf[span(step), :], 1, 1)
        d_buf[...] = dot(v_buf[...], g_buf[span(step), :], 1, 1)
        lane = lax.broadcasted_iota(jnp.int32, (8, ROWS), 1)
        sub = lax.broadcasted_iota(jnp.int32, (8, ROWS), 0)
        first = lane < BLOCK_LEN
        count_a, count_b = counts[source, 0], counts[source, 1]
        count = jnp.where(first, count_a, count_b)
        mask = jnp.full((8, ROWS), NEG_FILL, F32)
        for j in range(slots):
            picked = jnp.where(first, ids[source, 0, j], ids[source, 1, j])
            mask = jnp.where((picked == sub) & (count > j), 0.0, mask)

        def tile(p):
            return pl.ds(p * PASSAGE, PASSAGE)

        def group(x):
            return x.reshape(PASSAGE // 8, 8, ROWS)

        top = jnp.full((8, ROWS), 2 * NEG_FILL, F32)
        for p in range(pool):
            x = s_buf[tile(p), :] * (SCALE * LOG2E) + (bias_map[...] + mask[p : p + 1, :])
            s_buf[tile(p), :] = x
            top = jnp.maximum(top, jnp.max(group(x), axis=0))
        top = jnp.max(top, axis=0, keepdims=True)
        sums = jnp.zeros((8, ROWS), F32)
        dots = jnp.zeros((8, ROWS), F32)
        for p in range(pool):
            e = jnp.exp2(s_buf[tile(p), :] - top)
            s_buf[tile(p), :] = e
            sums = sums + jnp.sum(group(e), axis=0)
            dots = dots + jnp.sum(group(e * d_buf[tile(p), :]), axis=0)
        sums = jnp.sum(sums, axis=0, keepdims=True)
        inverse = jnp.where(count[0:1, :] > 0, 1.0 / sums, 0.0)
        delta = jnp.sum(dots, axis=0, keepdims=True) * inverse
        bias_here = bias_sum[...]
        for p in range(pool):
            w = s_buf[tile(p), :] * inverse
            ds = w * (d_buf[tile(p), :] - delta)
            w_all[tile(p), span(step)] = w.astype(BF16)
            ds_all[tile(p), span(step)] = ds.astype(BF16)
            bias_here = bias_here + ds
        bias_sum[...] = bias_here

    def give_back(step):
        c_turn = dot(v_turn[...], w_all[:, span(step)], 1, 0)
        c_buf[span(step), :] = c_turn.T.astype(BF16)
        dq_turn = dot(k_turn[...], ds_all[:, span(step)], 1, 0) * SCALE
        dq_buf[span(step), :] = dq_turn.T.astype(BF16)

    weigh(0)
    give_back(0)
    own = [
        pltpu.make_async_copy(c_buf.at[span(0)], context_out.at[0, :, span(enc)], own_sem.at[0]),
        pltpu.make_async_copy(dq_buf.at[span(0)], query_out.at[0, :, span(enc)], own_sem.at[1]),
    ]
    for copy in own:
        copy.start()

    def one_source(step):
        q_copy(step).wait_recv()
        g_copy(step).wait_recv()
        weigh(step)
        give_back(step)
        c_copy(step, enc).start()
        dq_copy(step, enc).start()

    each(1, n_enc, one_source)

    bias_row[...] = fold_bias(bias_sum[...])
    each(1, total, lambda step: b_copy(step, flat).start())

    dk_buf[...] = (dot(ds_all[...], q_buf[...], 1, 0) * SCALE).astype(BF16)
    key_store = pltpu.make_async_copy(dk_buf, key_out, store_sem.at[0])
    key_store.start()
    dv_buf[...] = dot(w_all[...], g_buf[...], 1, 0).astype(BF16)
    value_store = pltpu.make_async_copy(dv_buf, value_out, store_sem.at[1])
    value_store.start()

    parts[flat] = bias_row[...]

    def end_bias(step):
        b_copy(step, lax.rem(flat + (total - step), total)).wait_recv()

    each(1, total, end_bias)
    bias_total = parts[0]
    for place in range(1, total):
        bias_total = bias_total + parts[place]
    line[...] = bias_total[:, 0:table]
    bias_store = pltpu.make_async_copy(line, bias_out, store_sem.at[2])
    bias_store.start()

    def end_sends(step):
        q_copy(step).wait_send()
        g_copy(step).wait_send()
        c_copy(step, enc).wait_send()
        dq_copy(step, enc).wait_send()
        c_copy(step, to_peer(step)).wait_recv()
        dq_copy(step, to_peer(step)).wait_recv()

    each(1, n_enc, end_sends)
    each(1, total, lambda step: b_copy(step, flat).wait_send())
    for copy in own:
        copy.wait()
    key_store.wait()
    value_store.wait()
    bias_store.wait()


def local(n_dp, n_seq, n_enc, queries, cotangent, key_pool, value_pool, counts, neighbour_ids, rel_bias):
    pool = key_pool.shape[2]
    tokens = pool * PASSAGE
    slots = neighbour_ids.shape[-1]
    table = rel_bias.shape[1]
    total = n_dp * n_seq
    all_rows = n_enc * ROWS
    anywhere = pl.BlockSpec(memory_space=pl.ANY)
    context, query_grad, key_grad, value_grad, bias_grad = pl.pallas_call(
        functools.partial(kernel, n_dp, n_seq, n_enc, pool, slots),
        out_shape=[
            jax.ShapeDtypeStruct(queries.shape, BF16),
            jax.ShapeDtypeStruct(queries.shape, BF16),
            jax.ShapeDtypeStruct((tokens, HEAD_DIM), BF16),
            jax.ShapeDtypeStruct((tokens, HEAD_DIM), BF16),
            jax.ShapeDtypeStruct(rel_bias.shape, F32),
        ],
        in_specs=[anywhere] * 7,
        out_specs=[anywhere] * 5,
        scratch_shapes=[
            pltpu.VMEM((all_rows, HEAD_DIM), BF16),
            pltpu.VMEM((all_rows, HEAD_DIM), BF16),
            pltpu.VMEM((tokens, HEAD_DIM), BF16),
            pltpu.VMEM((tokens, HEAD_DIM), BF16),
            pltpu.VMEM((HEAD_DIM, tokens), BF16),
            pltpu.VMEM((HEAD_DIM, tokens), BF16),
            pltpu.SMEM(counts.shape, jnp.int32),
            pltpu.SMEM(neighbour_ids.shape, jnp.int32),
            pltpu.VMEM((1, table), F32),
            pltpu.VMEM((1, WIDE), F32),
            pltpu.VMEM((PASSAGE, ROWS), F32),
            pltpu.VMEM((tokens, ROWS), F32),
            pltpu.VMEM((tokens, ROWS), F32),
            pltpu.VMEM((tokens, all_rows), BF16),
            pltpu.VMEM((tokens, all_rows), BF16),
            pltpu.VMEM((PASSAGE, ROWS), F32),
            pltpu.VMEM((all_rows, HEAD_DIM), BF16),
            pltpu.VMEM((all_rows, HEAD_DIM), BF16),
            pltpu.VMEM((tokens, HEAD_DIM), BF16),
            pltpu.VMEM((tokens, HEAD_DIM), BF16),
            pltpu.VMEM((total, 1, WIDE), F32),
            pltpu.VMEM((1, WIDE), F32),
            pltpu.SemaphoreType.DMA((7,)),
            pltpu.SemaphoreType.DMA((2,)),
            pltpu.SemaphoreType.DMA((3,)),
        ]
        + [pltpu.SemaphoreType.DMA((n_enc,))] * 8
        + [pltpu.SemaphoreType.DMA((total,))] * 2,
        compiler_params=pltpu.CompilerParams(
            collective_id=0, has_side_effects=True, vmem_limit_bytes=48 * 1024 * 1024
        ),
        name="retrieval_attention",
    )(
        queries,
        cotangent,
        key_pool.reshape(tokens, HEAD_DIM),
        value_pool.reshape(tokens, HEAD_DIM),
        counts,
        neighbour_ids,
        rel_bias,
    )
    return (
        context,
        query_grad,
        key_grad.reshape(key_pool.shape),
        value_grad.reshape(value_pool.shape),
        bias_grad,
    )


def solution(mesh):
    in_specs = (
        P(("dp", "enc"), "seq", None),
        P(("dp", "enc"), "seq", None),
        P("dp", "seq", None, None, "enc"),
        P("dp", "seq", None, None, "enc"),
        P("dp", "seq"),
        P("dp", "seq", None),
        P("enc", None),
    )
    out_specs = (
        P(("dp", "enc"), "seq", None),
        P(("dp", "enc"), "seq", None),
        P("dp", "seq", None, None, "enc"),
        P("dp", "seq", None, None, "enc"),
        P("enc", None),
    )
    body = functools.partial(local, mesh.shape["dp"], mesh.shape["seq"], mesh.shape["enc"])
    return jax.shard_map(body, mesh=mesh, in_specs=in_specs, out_specs=out_specs, check_vma=False)
```

time: 73.8 us -> 24.2 us (0.33)
  blocking collectives: 22.8 us -> 0 us
  Pallas kernels: 0 us -> 15.6 us
  starting transfers between devices: 14.8 us -> 0 us
  other arithmetic: 11.1 us -> 0 us
  matrix products: 7.7 us -> 0 us
  local copies, waits for them, and re-layouts: 13 us -> 7.77 us
  waiting for transfers between devices: 2.67 us -> 0 us
    psum x1 -> x0, blocking collectives: 22.8 us -> none  [local(): lax.psum(fold_bias(bias_total, rel_bias.shape[1]), ('dp', 'seq'))]
    pallas_call x0 -> x1, Pallas kernels: none -> 15.6 us  [local(): pl.pallas_call(functools.partial(kernel, n_dp, n_seq, n_enc, pool, slots)...]
    all_to_all x4 -> x0, starting transfers between devices: 14.8 us -> none  [the longest x1 4.24 us: local(): lax.all_to_all(query_rows, 'enc', split_axis=2, concat_axis=0, tiled=True)]
    dot_general x6 -> x0, matrix products: 7.7 us -> none  [the longest x1 2.31 us: backward_one_batch(): jnp.einsum('chqjt,cqhd->cjthd', weights_low, grad_block, preferred_elemen...]
    scatter-add x2 -> x0, other arithmetic: 7.32 us -> none  [the longest x1 4.66 us: backward_one_batch(): value_total.at[flat_ids]]
    reshape x8 -> x0, local copies, waits for them, and re-layouts: 4.9 us -> none  [the longest x1 1.11 us: local(): query_rows = queries.reshape(blocks_here, BLOCK_LEN, full_width)]
    unnamed x15 -> x18, local copies, waits for them, and re-layouts: 3.02 us -> 7.77 us
    all_to_all x4 -> x0, waiting for transfers between devices: 2.67 us -> none  [the longest x1 2.66 us: local(): lax.all_to_all(grad_rows, 'enc', split_axis=2, concat_axis=0, tiled=True)]
  transfers between devices with their start and end apart: 4 -> 0, of which waited for: 1 -> 0; matrix products, arithmetic and copies ran while one was open for 30% -> 0% of each run, Pallas kernels for 0% -> 0%
where the time goes in v1:
time: 24.2 us; the launch traced here: 24 us
  Pallas kernels  15.6 us (64%)
  local copies, waits for them, and re-layouts  7.77 us (32%)
  between operations  0.66 us (3%)
    pallas_call x1, Pallas kernels, local(): pl.pallas_call(functools.partial(kernel, n_dp, n_seq, n_enc, pool, slots)...  15.6 us
    unnamed x18, local copies, waits for them, and re-layouts  7.77 us

profile of v1, /device:TPU:0, one launch (start us, length us, event | category | flops | bytes accessed | tf_op | source)
XLA Modules:
  0.0 24.0 jit_solution(7523691543002060848)
XLA Ops:
  0.6 0.0 copy-start.4
  0.6 0.0 copy-start.5
  0.7 0.8 %copy.12.count_hbm = s32[4,2]{1,0:T(4,128)S(1)} copy(s32[4,2]{0,1:T(2,128)} %param.11) | data formatting | bytes 64 | tf_op args[4]
  1.4 0.0 copy-done.4
  1.4 0.0 copy-done.5
  1.4 0.0 copy-start
  1.4 0.9 %copy-done = bf16[1,1,8,128,128]{4,3,2,1,0:T(8,128)(2,1)S(1)} copy-done((bf16[1,1,8,128,128]{4,3,2,1,0:T(8,128)(2,1)S(1)}, bf16[1,1,8,128,128]{4,3,2,1,0:T(8,128)(2,1)}, u32[]{:S(2)}) %copy-start) | copy-done | bytes 262168
  2.4 0.0 copy-start.1
  2.4 0.9 %copy-done.1 = bf16[1,1,8,128,128]{4,3,2,1,0:T(8,128)(2,1)S(1)} copy-done((bf16[1,1,8,128,128]{4,3,2,1,0:T(8,128)(2,1)S(1)}, bf16[1,1,8,128,128]{4,3,2,1,0:T(8,128)(2,1)}, u32[]{:S(2)}) %copy-start.1) | copy-done | bytes 262168
  3.3 0.0 copy-start.2
  3.3 0.9 %copy-done.2 = bf16[1,128,512]{2,1,0:T(8,128)(2,1)S(1)} copy-done((bf16[1,128,512]{2,1,0:T(8,128)(2,1)S(1)}, bf16[1,128,512]{2,1,0:T(8,128)(2,1)}, u32[]{:S(2)}) %copy-start.2) | copy-done | bytes 131096
  4.2 0.0 copy-start.3
  4.2 0.9 %copy-done.3 = bf16[1,128,512]{2,1,0:T(8,128)(2,1)S(1)} copy-done((bf16[1,128,512]{2,1,0:T(8,128)(2,1)S(1)}, bf16[1,128,512]{2,1,0:T(8,128)(2,1)}, u32[]{:S(2)}) %copy-start.3) | copy-done | bytes 131096
  5.1 15.6 %retrieval_attention.1 = (bf16[1,128,512]{2,1,0:T(8,128)(2,1)S(1)}, bf16[1,128,512]{2,1,0:T(8,128)(2,1)S(1)}, bf16[1024,128]{1,0:T(8,128)(2,1)S(1)}, bf16[1024,128]{1,0:T(8,128)(2,1)S(1)}, f32[1,191]{1,0:T(1,128)S(1)}) custom-call(bf16[1,128,512]{2,1,0:T(8,128)(2,1)S(1)} %copy-done.2, bf16[1,128,512]{2,1,0:T(8,128)(2,1)S(1)} %copy-done.3, ...), custom_call_target="tpu_custom_call" | custom-call | tf_op jit(solution)/shard_map/retrieval_attention/pallas_call | solution.py:292
  20.7 0.7 %copy.18 = bf16[1,128,512]{2,1,0:T(8,128)(2,1)} copy(bf16[1,128,512]{2,1,0:T(8,128)(2,1)S(1)} %get-tuple-element.20) | data formatting | bytes 262144
  21.4 0.7 %copy.19 = bf16[1,128,512]{2,1,0:T(8,128)(2,1)} copy(bf16[1,128,512]{2,1,0:T(8,128)(2,1)S(1)} %get-tuple-element.21) | data formatting | bytes 262144
  22.0 0.7 %copy.20 = bf16[1,1,8,128,128]{4,3,2,1,0:T(8,128)(2,1)} copy(bf16[1,1,8,128,128]{4,3,2,1,0:T(8,128)(2,1)S(1)} %bitcast.7) | data formatting | bytes 524288
  22.7 0.7 %copy.21 = bf16[1,1,8,128,128]{4,3,2,1,0:T(8,128)(2,1)} copy(bf16[1,1,8,128,128]{4,3,2,1,0:T(8,128)(2,1)S(1)} %bitcast.6) | data formatting | bytes 524288
  23.4 0.6 %copy.22 = f32[1,191]{1,0:T(1,128)} copy(f32[1,191]{1,0:T(1,128)S(1)} %get-tuple-element.24) | data formatting | bytes 1528
Async XLA Ops:
  0.6 0.8 %copy-start.4 = (s32[4,2,4]{2,1,0:T(2,128)S(1)}, s32[4,2,4]{2,1,0:T(2,128)}, u32[]{:S(2)}) copy-start(s32[4,2,4]{2,1,0:T(2,128)} %id_hbm.1) | copy-start | bytes 388
  0.6 0.8 %copy-start.5 = (f32[1,191]{1,0:T(1,128)S(1)}, f32[1,191]{1,0:T(1,128)}, u32[]{:S(2)}) copy-start(f32[1,191]{1,0:T(1,128)} %bias_hbm.1) | copy-start | bytes 2296
  1.4 1.0 %copy-start = (bf16[1,1,8,128,128]{4,3,2,1,0:T(8,128)(2,1)S(1)}, bf16[1,1,8,128,128]{4,3,2,1,0:T(8,128)(2,1)}, u32[]{:S(2)}) copy-start(bf16[1,1,8,128,128]{4,3,2,1,0:T(8,128)(2,1)} %param.9) | copy-start | bytes 786436
  2.4 0.9 %copy-start.1 = (bf16[1,1,8,128,128]{4,3,2,1,0:T(8,128)(2,1)S(1)}, bf16[1,1,8,128,128]{4,3,2,1,0:T(8,128)(2,1)}, u32[]{:S(2)}) copy-start(bf16[1,1,8,128,128]{4,3,2,1,0:T(8,128)(2,1)} %param.10) | copy-start | bytes 786436
  3.3 0.9 %copy-start.2 = (bf16[1,128,512]{2,1,0:T(8,128)(2,1)S(1)}, bf16[1,128,512]{2,1,0:T(8,128)(2,1)}, u32[]{:S(2)}) copy-start(bf16[1,128,512]{2,1,0:T(8,128)(2,1)} %q_hbm.1) | copy-start | bytes 393220
  4.2 0.9 %copy-start.3 = (bf16[1,128,512]{2,1,0:T(8,128)(2,1)S(1)}, bf16[1,128,512]{2,1,0:T(8,128)(2,1)}, u32[]{:S(2)}) copy-start(bf16[1,128,512]{2,1,0:T(8,128)(2,1)} %g_hbm.1) | copy-start | bytes 393220

commit v2 on v1

--- a/solution.py
+++ b/solution.py
@@ -84,11 +84,22 @@
     flat = dp * n_seq + seq
     table = line.shape[1]
 
+    paired = n_enc <= 8 and n_enc & (n_enc - 1) == 0
+
+    def partner(step):
+        place = enc
+        bit = 1
+        while bit < n_enc:
+            if step & bit:
+                place = place + bit * (1 - 2 * lax.rem(enc // bit, 2))
+            bit *= 2
+        return place
+
     def to_peer(step):
-        return lax.rem(enc + step, n_enc)
+        return partner(step) if paired else lax.rem(enc + step, n_enc)
 
     def from_peer(step):
-        return lax.rem(enc + (n_enc - step), n_enc)
+        return partner(step) if paired else lax.rem(enc + (n_enc - step), n_enc)
 
     def group_at(place):
         return (place // n_seq, lax.rem(place, n_seq), enc)
@@ -119,14 +130,6 @@
     loads = [pltpu.make_async_copy(a, b, load_sem.at[i]) for i, (a, b) in enumerate(loads)]
     for load in loads:
         load.start()
-    for load in loads[:3]:
-        load.wait()
-
-    wide_line[...] = jnp.zeros_like(wide_line)
-    wide_line[:, 0:table] = line[...]
-    bias_map[...] = spread_bias(wide_line[...])
-    bias_sum[...] = jnp.zeros_like(bias_sum)
-
     pl.semaphore_wait(barrier, n_enc - 1 + total - 1)
 
     def q_copy(step):
@@ -163,49 +166,62 @@
         q_copy(step).start()
         g_copy(step).start()
 
-    each(1, n_enc, send_inputs)
-
-    for load in loads[3:]:
+    each(1, n_enc, lambda step: send_inputs(n_enc - step))
+
+    for load in loads:
         load.wait()
+    wide_line[...] = jnp.zeros_like(wide_line)
+    wide_line[:, 0:table] = line[...]
+    bias_map[...] = spread_bias(wide_line[...])
+    bias_sum[...] = jnp.zeros_like(bias_sum)
     for p in range(pool):
         k_turn[:, p * PASSAGE : (p + 1) * PASSAGE] = k_buf[p * PASSAGE : (p + 1) * PASSAGE, :].T
         v_turn[:, p * PASSAGE : (p + 1) * PASSAGE] = v_buf[p * PASSAGE : (p + 1) * PASSAGE, :].T
 
     def weigh(step):
         source = from_peer(step)
-        s_buf[...] = dot(k_buf[...], q_buf[span(step), :], 1, 1)
-        d_buf[...] = dot(v_buf[...], g_buf[span(step), :], 1, 1)
+        query, grad = q_buf[span(step), :], g_buf[span(step), :]
         lane = lax.broadcasted_iota(jnp.int32, (8, ROWS), 1)
         sub = lax.broadcasted_iota(jnp.int32, (8, ROWS), 0)
         first = lane < BLOCK_LEN
-        count_a, count_b = counts[source, 0], counts[source, 1]
+        count_a, count_b = counts[0, source], counts[1, source]
         count = jnp.where(first, count_a, count_b)
         mask = jnp.full((8, ROWS), NEG_FILL, F32)
         for j in range(slots):
             picked = jnp.where(first, ids[source, 0, j], ids[source, 1, j])
             mask = jnp.where((picked == sub) & (count > j), 0.0, mask)
 
+        live = count[0:1, :] > 0
+
         def tile(p):
             return pl.ds(p * PASSAGE, PASSAGE)
 
         def group(x):
             return x.reshape(PASSAGE // 8, 8, ROWS)
 
-        top = jnp.full((8, ROWS), 2 * NEG_FILL, F32)
-        for p in range(pool):
-            x = s_buf[tile(p), :] * (SCALE * LOG2E) + (bias_map[...] + mask[p : p + 1, :])
-            s_buf[tile(p), :] = x
-            top = jnp.maximum(top, jnp.max(group(x), axis=0))
-        top = jnp.max(top, axis=0, keepdims=True)
+        top = jnp.full((1, ROWS), 2 * NEG_FILL, F32)
+        for pair in range(0, pool, 2):
+            raw = dot(k_buf[pl.ds(pair * PASSAGE, 2 * PASSAGE), :], query, 1, 1)
+            for p in (pair, pair + 1):
+                x = raw[(p - pair) * PASSAGE : (p - pair + 1) * PASSAGE]
+                x = x * (SCALE * LOG2E) + bias_map[...]
+                s_buf[tile(p), :] = x
+                highest = jnp.max(jnp.max(group(x), axis=0), axis=0, keepdims=True)
+                top = jnp.maximum(top, highest + mask[p : p + 1, :])
+        shift = mask - jnp.where(live, top, 0.0)
         sums = jnp.zeros((8, ROWS), F32)
         dots = jnp.zeros((8, ROWS), F32)
-        for p in range(pool):
-            e = jnp.exp2(s_buf[tile(p), :] - top)
-            s_buf[tile(p), :] = e
-            sums = sums + jnp.sum(group(e), axis=0)
-            dots = dots + jnp.sum(group(e * d_buf[tile(p), :]), axis=0)
+        for pair in range(0, pool, 2):
+            raw = dot(v_buf[pl.ds(pair * PASSAGE, 2 * PASSAGE), :], grad, 1, 1)
+            for p in (pair, pair + 1):
+                d = raw[(p - pair) * PASSAGE : (p - pair + 1) * PASSAGE]
+                e = jnp.exp2(s_buf[tile(p), :] + shift[p : p + 1, :])
+                s_buf[tile(p), :] = e
+                d_buf[tile(p), :] = d
+                sums = sums + jnp.sum(group(e), axis=0)
+                dots = dots + jnp.sum(group(e * d), axis=0)
         sums = jnp.sum(sums, axis=0, keepdims=True)
-        inverse = jnp.where(count[0:1, :] > 0, 1.0 / sums, 0.0)
+        inverse = jnp.where(live, 1.0 / sums, 0.0)
         delta = jnp.sum(dots, axis=0, keepdims=True) * inverse
         bias_here = bias_sum[...]
         for p in range(pool):
@@ -231,18 +247,25 @@
     for copy in own:
         copy.start()
 
-    def one_source(step):
+    def arrive(step):
         q_copy(step).wait_recv()
         g_copy(step).wait_recv()
-        weigh(step)
+
+    def reply(step):
         give_back(step)
         c_copy(step, enc).start()
         dq_copy(step, enc).start()
 
-    each(1, n_enc, one_source)
-
+    def one_source(step):
+        weigh(step)
+        reply(step)
+
+    each(1, n_enc, arrive)
+    each(2, n_enc, lambda step: one_source(n_enc + 1 - step))
+    weigh(1)
     bias_row[...] = fold_bias(bias_sum[...])
     each(1, total, lambda step: b_copy(step, flat).start())
+    reply(1)
 
     dk_buf[...] = (dot(ds_all[...], q_buf[...], 1, 0) * SCALE).astype(BF16)
     key_store = pltpu.make_async_copy(dk_buf, key_out, store_sem.at[0])
@@ -279,6 +302,18 @@
     key_store.wait()
     value_store.wait()
     bias_store.wait()
+
+
+def write_out(*refs):
+    sources, targets, sem = refs[:5], refs[5:10], refs[10]
+    copies = [
+        pltpu.make_async_copy(source, target, sem.at[i])
+        for i, (source, target) in enumerate(zip(sources, targets))
+    ]
+    for copy in copies:
+        copy.start()
+    for copy in copies:
+        copy.wait()
 
 
 def local(n_dp, n_seq, n_enc, queries, cotangent, key_pool, value_pool, counts, neighbour_ids, rel_bias):
@@ -289,7 +324,8 @@
     total = n_dp * n_seq
     all_rows = n_enc * ROWS
     anywhere = pl.BlockSpec(memory_space=pl.ANY)
-    context, query_grad, key_grad, value_grad, bias_grad = pl.pallas_call(
+    held = pl.BlockSpec(memory_space=pltpu.HBM)
+    results = pl.pallas_call(
         functools.partial(kernel, n_dp, n_seq, n_enc, pool, slots),
         out_shape=[
             jax.ShapeDtypeStruct(queries.shape, BF16),
@@ -298,7 +334,7 @@
             jax.ShapeDtypeStruct((tokens, HEAD_DIM), BF16),
             jax.ShapeDtypeStruct(rel_bias.shape, F32),
         ],
-        in_specs=[anywhere] * 7,
+        in_specs=[held] * 7,
         out_specs=[anywhere] * 5,
         scratch_shapes=[
             pltpu.VMEM((all_rows, HEAD_DIM), BF16),
@@ -307,7 +343,7 @@
             pltpu.VMEM((tokens, HEAD_DIM), BF16),
             pltpu.VMEM((HEAD_DIM, tokens), BF16),
             pltpu.VMEM((HEAD_DIM, tokens), BF16),
-            pltpu.SMEM(counts.shape, jnp.int32),
+            pltpu.SMEM(counts.shape[::-1], jnp.int32),
             pltpu.SMEM(neighbour_ids.shape, jnp.int32),
             pltpu.VMEM((1, table), F32),
             pltpu.VMEM((1, WIDE), F32),
@@ -334,14 +370,22 @@
         ),
         name="retrieval_attention",
     )(
-        queries,
-        cotangent,
-        key_pool.reshape(tokens, HEAD_DIM),
-        value_pool.reshape(tokens, HEAD_DIM),
-        counts,
-        neighbour_ids,
-        rel_bias,
+        pltpu.with_memory_space_constraint(queries, pltpu.HBM),
+        pltpu.with_memory_space_constraint(cotangent, pltpu.HBM),
+        pltpu.with_memory_space_constraint(key_pool.reshape(tokens, HEAD_DIM), pltpu.HBM),
+        pltpu.with_memory_space_constraint(value_pool.reshape(tokens, HEAD_DIM), pltpu.HBM),
+        pltpu.with_memory_space_constraint(counts.T, pltpu.HBM),
+        pltpu.with_memory_space_constraint(neighbour_ids, pltpu.HBM),
+        pltpu.with_memory_space_constraint(rel_bias, pltpu.HBM),
     )
+    context, query_grad, key_grad, value_grad, bias_grad = pl.pallas_call(
+        write_out,
+        out_shape=[jax.ShapeDtypeStruct(x.shape, x.dtype) for x in results],
+        in_specs=[anywhere] * 5,
+        out_specs=[held] * 5,
+        scratch_shapes=[pltpu.SemaphoreType.DMA((5,))],
+        name="write_out",
+    )(*results)
     return (
         context,
         query_grad,

time: 24.2 us -> 46.1 us (1.90)
  Pallas kernels: 15.6 us -> 42 us
  local copies, waits for them, and re-layouts: 7.77 us -> 3.26 us
    pallas_call x0 -> x1, Pallas kernels: none -> 25 us  [local(): pl.pallas_call(write_out, out_shape=[jax.ShapeDtypeStruct(x.shape, x.dtyp...]
    unnamed x18 -> x10, local copies, waits for them, and re-layouts: 7.77 us -> 3.26 us
    pallas_call x1, Pallas kernels: 15.6 us -> 17 us  [local(): pl.pallas_call(functools.partial(kernel, n_dp, n_seq, n_enc, pool, slots)...]
where the time goes in v2:
time: 46.1 us; the launch traced here: 45.9 us
  Pallas kernels  42 us (91%)
  local copies, waits for them, and re-layouts  3.26 us (7%)
  between operations  0.65 us (1%)
    pallas_call x1, Pallas kernels, local(): pl.pallas_call(write_out, out_shape=[jax.ShapeDtypeStruct(x.shape, x.dtyp...  25 us
    pallas_call x1, Pallas kernels, local(): pl.pallas_call(functools.partial(kernel, n_dp, n_seq, n_enc, pool, slots)...  17 us
    unnamed x10, local copies, waits for them, and re-layouts  3.26 us

profile of v2, /device:TPU:0, one launch (start us, length us, event | category | flops | bytes accessed | tf_op | source)
XLA Modules:
  0.0 45.9 jit_solution(17556095690534041089)
XLA Ops:
  0.6 17.0 %retrieval_attention.1 = (bf16[1,128,512]{2,1,0:T(8,128)(2,1)S(1)}, bf16[1,128,512]{2,1,0:T(8,128)(2,1)S(1)}, bf16[1024,128]{1,0:T(8,128)(2,1)S(1)}, bf16[1024,128]{1,0:T(8,128)(2,1)S(1)}, f32[1,191]{1,0:T(1,128)S(1)}) custom-call(bf16[1,128,512]{2,1,0:T(8,128)(2,1)} %q_hbm.1, bf16[1,128,512]{2,1,0:T(8,128)(2,1)} %g_hbm.1, bf16[1024,128]{1,0:T(8,128)(2,1)} %bitcast.5, ...), custom_call_target="tpu_custom_call" | custom-call | tf_op jit(solution)/shard_map/retrieval_attention/pallas_call | solution.py:328
  17.7 0.0 copy-start
  17.7 0.7 %copy-done = bf16[1024,128]{1,0:T(8,128)(2,1)} copy-done((bf16[1024,128]{1,0:T(8,128)(2,1)}, bf16[1024,128]{1,0:T(8,128)(2,1)S(1)}, u32[]{:S(2)}) %copy-start) | copy-done | bytes 262168
  18.4 0.0 copy-start.1
  18.4 0.7 %copy-done.1 = bf16[1024,128]{1,0:T(8,128)(2,1)} copy-done((bf16[1024,128]{1,0:T(8,128)(2,1)}, bf16[1024,128]{1,0:T(8,128)(2,1)S(1)}, u32[]{:S(2)}) %copy-start.1) | copy-done | bytes 262168
  19.1 0.0 copy-start.2
  19.1 0.6 %copy-done.2 = bf16[1,128,512]{2,1,0:T(8,128)(2,1)} copy-done((bf16[1,128,512]{2,1,0:T(8,128)(2,1)}, bf16[1,128,512]{2,1,0:T(8,128)(2,1)S(1)}, u32[]{:S(2)}) %copy-start.2) | copy-done | bytes 131096
  19.7 0.0 copy-start.3
  19.7 0.6 %copy-done.3 = bf16[1,128,512]{2,1,0:T(8,128)(2,1)} copy-done((bf16[1,128,512]{2,1,0:T(8,128)(2,1)}, bf16[1,128,512]{2,1,0:T(8,128)(2,1)S(1)}, u32[]{:S(2)}) %copy-start.3) | copy-done | bytes 131096
  20.4 0.0 copy-start.4
  20.4 0.6 %copy-done.4 = f32[1,191]{1,0:T(1,128)} copy-done((f32[1,191]{1,0:T(1,128)}, f32[1,191]{1,0:T(1,128)S(1)}, u32[]{:S(2)}) %copy-start.4) | copy-done | bytes 788
  20.9 25.0 %write_out.1 = (bf16[1,128,512]{2,1,0:T(8,128)(2,1)}, bf16[1,128,512]{2,1,0:T(8,128)(2,1)}, bf16[1024,128]{1,0:T(8,128)(2,1)}, bf16[1024,128]{1,0:T(8,128)(2,1)}, f32[1,191]{1,0:T(1,128)}) custom-call(bf16[1,128,512]{2,1,0:T(8,128)(2,1)} %copy-done.2, bf16[1,128,512]{2,1,0:T(8,128)(2,1)} %copy-done.3, bf16[1024,128]{1,0:T(8,128)(2,1)} %copy-done, ...), custom_call_target="tpu_custom_call" | custom-call | tf_op jit(solution)/shard_map/write_out/pallas_call | solution.py:381
Async XLA Ops:
  17.7 0.7 %copy-start = (bf16[1024,128]{1,0:T(8,128)(2,1)}, bf16[1024,128]{1,0:T(8,128)(2,1)S(1)}, u32[]{:S(2)}) copy-start(bf16[1024,128]{1,0:T(8,128)(2,1)S(1)} %get-tuple-element.17.refs_2_) | copy-start | bytes 786436
  18.4 0.7 %copy-start.1 = (bf16[1024,128]{1,0:T(8,128)(2,1)}, bf16[1024,128]{1,0:T(8,128)(2,1)S(1)}, u32[]{:S(2)}) copy-start(bf16[1024,128]{1,0:T(8,128)(2,1)S(1)} %get-tuple-element.18.refs_3_) | copy-start | bytes 786436
  19.1 0.6 %copy-start.2 = (bf16[1,128,512]{2,1,0:T(8,128)(2,1)}, bf16[1,128,512]{2,1,0:T(8,128)(2,1)S(1)}, u32[]{:S(2)}) copy-start(bf16[1,128,512]{2,1,0:T(8,128)(2,1)S(1)} %get-tuple-element.15.refs_0_) | copy-start | bytes 393220
  19.7 0.6 %copy-start.3 = (bf16[1,128,512]{2,1,0:T(8,128)(2,1)}, bf16[1,128,512]{2,1,0:T(8,128)(2,1)S(1)}, u32[]{:S(2)}) copy-start(bf16[1,128,512]{2,1,0:T(8,128)(2,1)S(1)} %get-tuple-element.16.refs_1_) | copy-start | bytes 393220
  20.4 0.6 %copy-start.4 = (f32[1,191]{1,0:T(1,128)}, f32[1,191]{1,0:T(1,128)S(1)}, u32[]{:S(2)}) copy-start(f32[1,191]{1,0:T(1,128)S(1)} %get-tuple-element.19.refs_4_) | copy-start | bytes 2296

commit v3 on v2

--- a/solution.py
+++ b/solution.py
@@ -22,8 +22,8 @@
 MESH = pl.DeviceIdType.MESH
 
 
-def each(low, high, body):
-    if high - low <= 8:
+def each(low, high, body, unrolled=8):
+    if high - low <= unrolled:
         for step in range(low, high):
             body(step)
     else:
@@ -35,10 +35,10 @@
         lax.fori_loop(low, high, one, 0)
 
 
-def span(index):
+def span(index, width=1):
     if isinstance(index, int):
-        return pl.ds(index * ROWS, ROWS)
-    return pl.ds(pl.multiple_of(index * ROWS, ROWS), ROWS)
+        return pl.ds(index * ROWS, width * ROWS)
+    return pl.ds(pl.multiple_of(index * ROWS, ROWS), width * ROWS)
 
 
 def dot(left, right, left_dim, right_dim):
@@ -59,7 +59,8 @@
 
 
 def fold_bias(total):
-    turned = total.T
+    parts = [total[:, at : at + ROWS] for at in range(0, total.shape[1], ROWS)]
+    turned = functools.reduce(jnp.add, parts).T
     block = turned[:BLOCK_LEN] + turned[BLOCK_LEN:]
     block = jnp.concatenate([block, jnp.zeros((BLOCK_LEN, WIDE - PASSAGE), F32)], axis=1)
     for half in (32, 16, 8):
@@ -84,6 +85,8 @@
     flat = dp * n_seq + seq
     table = line.shape[1]
 
+    together = 2 if n_enc % 2 == 0 else 1
+    groups = n_enc // together
     paired = n_enc <= 8 and n_enc & (n_enc - 1) == 0
 
     def partner(step):
@@ -172,34 +175,43 @@
         load.wait()
     wide_line[...] = jnp.zeros_like(wide_line)
     wide_line[:, 0:table] = line[...]
-    bias_map[...] = spread_bias(wide_line[...])
+    bias_one = spread_bias(wide_line[...])
+    for at in range(together):
+        bias_map[:, span(at)] = bias_one
     bias_sum[...] = jnp.zeros_like(bias_sum)
     for p in range(pool):
         k_turn[:, p * PASSAGE : (p + 1) * PASSAGE] = k_buf[p * PASSAGE : (p + 1) * PASSAGE, :].T
         v_turn[:, p * PASSAGE : (p + 1) * PASSAGE] = v_buf[p * PASSAGE : (p + 1) * PASSAGE, :].T
 
-    def weigh(step):
+    def allowed(step):
         source = from_peer(step)
-        query, grad = q_buf[span(step), :], g_buf[span(step), :]
         lane = lax.broadcasted_iota(jnp.int32, (8, ROWS), 1)
         sub = lax.broadcasted_iota(jnp.int32, (8, ROWS), 0)
         first = lane < BLOCK_LEN
-        count_a, count_b = counts[0, source], counts[1, source]
-        count = jnp.where(first, count_a, count_b)
+        count = jnp.where(first, counts[0, source], counts[1, source])
         mask = jnp.full((8, ROWS), NEG_FILL, F32)
         for j in range(slots):
             picked = jnp.where(first, ids[source, 0, j], ids[source, 1, j])
             mask = jnp.where((picked == sub) & (count > j), 0.0, mask)
-
+        return mask, count
+
+    def weigh(batch):
+        at = batch * together
+        here = span(at, together)
+        columns = together * ROWS
+        query, grad = q_buf[here, :], g_buf[here, :]
+        masks = [allowed(at + k) for k in range(together)]
+        mask = jnp.concatenate([pair[0] for pair in masks], axis=1)
+        count = jnp.concatenate([pair[1] for pair in masks], axis=1)
         live = count[0:1, :] > 0
 
         def tile(p):
             return pl.ds(p * PASSAGE, PASSAGE)
 
         def group(x):
-            return x.reshape(PASSAGE // 8, 8, ROWS)
-
-        top = jnp.full((1, ROWS), 2 * NEG_FILL, F32)
+            return x.reshape(PASSAGE // 8, 8, columns)
+
+        top = jnp.full((1, columns), 2 * NEG_FILL, F32)
         for pair in range(0, pool, 2):
             raw = dot(k_buf[pl.ds(pair * PASSAGE, 2 * PASSAGE), :], query, 1, 1)
             for p in (pair, pair + 1):
@@ -209,8 +221,8 @@
                 highest = jnp.max(jnp.max(group(x), axis=0), axis=0, keepdims=True)
                 top = jnp.maximum(top, highest + mask[p : p + 1, :])
         shift = mask - jnp.where(live, top, 0.0)
-        sums = jnp.zeros((8, ROWS), F32)
-        dots = jnp.zeros((8, ROWS), F32)
+        sums = jnp.zeros((8, columns), F32)
+        dots = jnp.zeros((8, columns), F32)
         for pair in range(0, pool, 2):
             raw = dot(v_buf[pl.ds(pair * PASSAGE, 2 * PASSAGE), :], grad, 1, 1)
             for p in (pair, pair + 1):
@@ -227,19 +239,35 @@
         for p in range(pool):
             w = s_buf[tile(p), :] * inverse
             ds = w * (d_buf[tile(p), :] - delta)
-            w_all[tile(p), span(step)] = w.astype(BF16)
-            ds_all[tile(p), span(step)] = ds.astype(BF16)
+            w_all[tile(p), here] = w.astype(BF16)
+            ds_all[tile(p), here] = ds.astype(BF16)
             bias_here = bias_here + ds
         bias_sum[...] = bias_here
 
-    def give_back(step):
-        c_turn = dot(v_turn[...], w_all[:, span(step)], 1, 0)
-        c_buf[span(step), :] = c_turn.T.astype(BF16)
-        dq_turn = dot(k_turn[...], ds_all[:, span(step)], 1, 0) * SCALE
-        dq_buf[span(step), :] = dq_turn.T.astype(BF16)
-
-    weigh(0)
-    give_back(0)
+    def give_back(batch):
+        here = span(batch * together, together)
+        c_turn = dot(v_turn[...], w_all[:, here], 1, 0)
+        c_buf[here, :] = c_turn.T.astype(BF16)
+        each_of(batch, lambda step: c_copy(step, enc).start())
+        dq_turn = dot(k_turn[...], ds_all[:, here], 1, 0) * SCALE
+        dq_buf[here, :] = dq_turn.T.astype(BF16)
+        each_of(batch, lambda step: dq_copy(step, enc).start())
+
+    def each_of(batch, body):
+        for k in range(together):
+            if not (isinstance(batch, int) and batch * together + k == 0):
+                body(batch * together + k)
+
+    def arrive(step):
+        q_copy(step).wait_recv()
+        g_copy(step).wait_recv()
+
+    def one_batch(batch):
+        each_of(batch, arrive)
+        weigh(batch)
+        give_back(batch)
+
+    one_batch(0)
     own = [
         pltpu.make_async_copy(c_buf.at[span(0)], context_out.at[0, :, span(enc)], own_sem.at[0]),
         pltpu.make_async_copy(dq_buf.at[span(0)], query_out.at[0, :, span(enc)], own_sem.at[1]),
@@ -247,25 +275,18 @@
     for copy in own:
         copy.start()
 
-    def arrive(step):
-        q_copy(step).wait_recv()
-        g_copy(step).wait_recv()
-
-    def reply(step):
-        give_back(step)
-        c_copy(step, enc).start()
-        dq_copy(step, enc).start()
-
-    def one_source(step):
-        weigh(step)
-        reply(step)
-
-    each(1, n_enc, arrive)
-    each(2, n_enc, lambda step: one_source(n_enc + 1 - step))
-    weigh(1)
-    bias_row[...] = fold_bias(bias_sum[...])
-    each(1, total, lambda step: b_copy(step, flat).start())
-    reply(1)
+    def send_bias():
+        bias_row[...] = fold_bias(bias_sum[...])
+        each(1, total, lambda step: b_copy(step, flat).start())
+
+    last = groups - 1
+    each(1, last, one_batch, unrolled=2)
+    if last > 0:
+        each_of(last, arrive)
+        weigh(last)
+    send_bias()
+    if last > 0:
+        give_back(last)
 
     dk_buf[...] = (dot(ds_all[...], q_buf[...], 1, 0) * SCALE).astype(BF16)
     key_store = pltpu.make_async_copy(dk_buf, key_out, store_sem.at[0])
@@ -323,6 +344,7 @@
     table = rel_bias.shape[1]
     total = n_dp * n_seq
     all_rows = n_enc * ROWS
+    batch_rows = ROWS * (2 if n_enc % 2 == 0 else 1)
     anywhere = pl.BlockSpec(memory_space=pl.ANY)
     held = pl.BlockSpec(memory_space=pltpu.HBM)
     results = pl.pallas_call(
@@ -347,12 +369,12 @@
             pltpu.SMEM(neighbour_ids.shape, jnp.int32),
             pltpu.VMEM((1, table), F32),
             pltpu.VMEM((1, WIDE), F32),
-            pltpu.VMEM((PASSAGE, ROWS), F32),
-            pltpu.VMEM((tokens, ROWS), F32),
-            pltpu.VMEM((tokens, ROWS), F32),
+            pltpu.VMEM((PASSAGE, batch_rows), F32),
+            pltpu.VMEM((tokens, batch_rows), F32),
+            pltpu.VMEM((tokens, batch_rows), F32),
             pltpu.VMEM((tokens, all_rows), BF16),
             pltpu.VMEM((tokens, all_rows), BF16),
-            pltpu.VMEM((PASSAGE, ROWS), F32),
+            pltpu.VMEM((PASSAGE, batch_rows), F32),
             pltpu.VMEM((all_rows, HEAD_DIM), BF16),
             pltpu.VMEM((all_rows, HEAD_DIM), BF16),
             pltpu.VMEM((tokens, HEAD_DIM), BF16),
@@ -384,6 +406,7 @@
         in_specs=[anywhere] * 5,
         out_specs=[held] * 5,
         scratch_shapes=[pltpu.SemaphoreType.DMA((5,))],
+        compiler_params=pltpu.CompilerParams(vmem_limit_bytes=2 * 1024 * 1024),
         name="write_out",
     )(*results)
     return (

time: 46.1 us -> 18.1 us (0.39)
  Pallas kernels: 42 us -> 17.3 us
  local copies, waits for them, and re-layouts: 3.26 us -> 0 us
    pallas_call x1, Pallas kernels: 25 us -> 0.92 us  [local(): pl.pallas_call(write_out, out_shape=[jax.ShapeDtypeStruct(x.shape, x.dtyp...]
    unnamed x10 -> x0, local copies, waits for them, and re-layouts: 3.26 us -> none
    pallas_call x1, Pallas kernels: 17 us -> 16.3 us  [local(): pl.pallas_call(functools.partial(kernel, n_dp, n_seq, n_enc, pool, slots)...]
where the time goes in v3:
time: 18.1 us; the launch traced here: 17.9 us
  Pallas kernels  17.3 us (96%)
  between operations  0.64 us (4%)
    pallas_call x1, Pallas kernels, local(): pl.pallas_call(functools.partial(kernel, n_dp, n_seq, n_enc, pool, slots)...  16.3 us
    pallas_call x1, Pallas kernels, local(): pl.pallas_call(write_out, out_shape=[jax.ShapeDtypeStruct(x.shape, x.dtyp...  0.92 us

profile of v3, /device:TPU:0, one launch (start us, length us, event | category | flops | bytes accessed | tf_op | source)
XLA Modules:
  0.0 17.9 jit_solution(5301233021660877764)
XLA Ops:
  0.6 16.3 %retrieval_attention.1 = (bf16[1,128,512]{2,1,0:T(8,128)(2,1)S(1)}, bf16[1,128,512]{2,1,0:T(8,128)(2,1)S(1)}, bf16[1024,128]{1,0:T(8,128)(2,1)S(1)}, bf16[1024,128]{1,0:T(8,128)(2,1)S(1)}, f32[1,191]{1,0:T(1,128)S(1)}) custom-call(bf16[1,128,512]{2,1,0:T(8,128)(2,1)} %q_hbm.1, bf16[1,128,512]{2,1,0:T(8,128)(2,1)} %g_hbm.1, bf16[1024,128]{1,0:T(8,128)(2,1)} %bitcast.5, ...), custom_call_target="tpu_custom_call" | custom-call | tf_op jit(solution)/shard_map/retrieval_attention/pallas_call | solution.py:350
  17.0 0.9 %write_out.1 = (bf16[1,128,512]{2,1,0:T(8,128)(2,1)}, bf16[1,128,512]{2,1,0:T(8,128)(2,1)}, bf16[1024,128]{1,0:T(8,128)(2,1)}, bf16[1024,128]{1,0:T(8,128)(2,1)}, f32[1,191]{1,0:T(1,128)}) custom-call(bf16[1,128,512]{2,1,0:T(8,128)(2,1)S(1)} %get-tuple-element.15.refs_0_, bf16[1,128,512]{2,1,0:T(8,128)(2,1)S(1)} %get-tuple-element.16.refs_1_, ...), custom_call_target="tpu_custom_call" | custom-call | tf_op jit(solution)/shard_map/write_out/pallas_call | solution.py:403

commit v4 on v3

--- a/solution.py
+++ b/solution.py
@@ -16,7 +16,6 @@
 
 NEG_FILL = -1e30
 SCALE = 1.0 / math.sqrt(HEAD_DIM)
-LOG2E = math.log2(math.e)
 F32 = jnp.float32
 BF16 = jnp.bfloat16
 MESH = pl.DeviceIdType.MESH
@@ -48,7 +47,7 @@
 
 
 def spread_bias(line):
-    rows = jnp.broadcast_to(line * LOG2E, (8, WIDE))
+    rows = jnp.broadcast_to(line, (8, WIDE))
     sub = lax.broadcasted_iota(jnp.int32, (8, WIDE), 0)
     rows = pltpu.roll(rows, WIDE - (BLOCK_LEN - 1), 1)
     for bit in (1, 2, 4):
@@ -211,38 +210,36 @@
         def group(x):
             return x.reshape(PASSAGE // 8, 8, columns)
 
-        top = jnp.full((1, columns), 2 * NEG_FILL, F32)
-        for pair in range(0, pool, 2):
-            raw = dot(k_buf[pl.ds(pair * PASSAGE, 2 * PASSAGE), :], query, 1, 1)
-            for p in (pair, pair + 1):
-                x = raw[(p - pair) * PASSAGE : (p - pair + 1) * PASSAGE]
-                x = x * (SCALE * LOG2E) + bias_map[...]
-                s_buf[tile(p), :] = x
-                highest = jnp.max(jnp.max(group(x), axis=0), axis=0, keepdims=True)
-                top = jnp.maximum(top, highest + mask[p : p + 1, :])
+        top = jnp.full((8, columns), 2 * NEG_FILL, F32)
+        for p in range(pool):
+            x = dot(k_buf[tile(p), :], query, 1, 1) * SCALE + bias_map[...]
+            s_buf[tile(p), :] = x
+            top = jnp.maximum(top, jnp.max(group(x), axis=0) + mask[p : p + 1, :])
+        top = jnp.max(top, axis=0, keepdims=True)
         shift = mask - jnp.where(live, top, 0.0)
         sums = jnp.zeros((8, columns), F32)
         dots = jnp.zeros((8, columns), F32)
-        for pair in range(0, pool, 2):
-            raw = dot(v_buf[pl.ds(pair * PASSAGE, 2 * PASSAGE), :], grad, 1, 1)
-            for p in (pair, pair + 1):
-                d = raw[(p - pair) * PASSAGE : (p - pair + 1) * PASSAGE]
-                e = jnp.exp2(s_buf[tile(p), :] + shift[p : p + 1, :])
-                s_buf[tile(p), :] = e
-                d_buf[tile(p), :] = d
-                sums = sums + jnp.sum(group(e), axis=0)
-                dots = dots + jnp.sum(group(e * d), axis=0)
+        for p in range(pool):
+            d = dot(v_buf[tile(p), :], grad, 1, 1)
+            e = jnp.exp(s_buf[tile(p), :] + shift[p : p + 1, :])
+            s_buf[tile(p), :] = e
+            d_buf[tile(p), :] = d
+            sums = sums + jnp.sum(group(e), axis=0)
+            dots = dots + jnp.sum(group(e * d), axis=0)
         sums = jnp.sum(sums, axis=0, keepdims=True)
         inverse = jnp.where(live, 1.0 / sums, 0.0)
         delta = jnp.sum(dots, axis=0, keepdims=True) * inverse
-        bias_here = bias_sum[...]
-        for p in range(pool):
-            w = s_buf[tile(p), :] * inverse
-            ds = w * (d_buf[tile(p), :] - delta)
-            w_all[tile(p), here] = w.astype(BF16)
-            ds_all[tile(p), here] = ds.astype(BF16)
-            bias_here = bias_here + ds
-        bias_sum[...] = bias_here
+        piece = 32
+        for low in range(0, PASSAGE, piece):
+            bias_here = bias_sum[low : low + piece, :]
+            for p in range(pool):
+                rows = pl.ds(p * PASSAGE + low, piece)
+                w = s_buf[rows, :] * inverse
+                ds = w * (d_buf[rows, :] - delta)
+                w_all[rows, here] = w.astype(BF16)
+                ds_all[rows, here] = ds.astype(BF16)
+                bias_here = bias_here + ds
+            bias_sum[low : low + piece, :] = bias_here
 
     def give_back(batch):
         here = span(batch * together, together)

time: 18.1 us -> 18.1 us (level)
  no operation moved by 1% of the time
where the time goes in v4:
time: 18.1 us; the launch traced here: 17.9 us
  Pallas kernels  17.3 us (96%)
  between operations  0.64 us (4%)
    pallas_call x1, Pallas kernels, local(): pl.pallas_call(functools.partial(kernel, n_dp, n_seq, n_enc, pool, slots)...  16.3 us
    pallas_call x1, Pallas kernels, local(): pl.pallas_call(write_out, out_shape=[jax.ShapeDtypeStruct(x.shape, x.dtyp...  0.92 us

profile of v4, /device:TPU:0, one launch (start us, length us, event | category | flops | bytes accessed | tf_op | source)
XLA Modules:
  0.0 17.9 jit_solution(11808580191436247064)
XLA Ops:
  0.6 16.3 %retrieval_attention.1 = (bf16[1,128,512]{2,1,0:T(8,128)(2,1)S(1)}, bf16[1,128,512]{2,1,0:T(8,128)(2,1)S(1)}, bf16[1024,128]{1,0:T(8,128)(2,1)S(1)}, bf16[1024,128]{1,0:T(8,128)(2,1)S(1)}, f32[1,191]{1,0:T(1,128)S(1)}) custom-call(bf16[1,128,512]{2,1,0:T(8,128)(2,1)} %q_hbm.1, bf16[1,128,512]{2,1,0:T(8,128)(2,1)} %g_hbm.1, bf16[1024,128]{1,0:T(8,128)(2,1)} %bitcast.5, ...), custom_call_target="tpu_custom_call" | custom-call | tf_op jit(solution)/shard_map/retrieval_attention/pallas_call | solution.py:347
  17.0 0.9 %write_out.1 = (bf16[1,128,512]{2,1,0:T(8,128)(2,1)}, bf16[1,128,512]{2,1,0:T(8,128)(2,1)}, bf16[1024,128]{1,0:T(8,128)(2,1)}, bf16[1024,128]{1,0:T(8,128)(2,1)}, f32[1,191]{1,0:T(1,128)}) custom-call(bf16[1,128,512]{2,1,0:T(8,128)(2,1)S(1)} %get-tuple-element.15.refs_0_, bf16[1,128,512]{2,1,0:T(8,128)(2,1)S(1)} %get-tuple-element.16.refs_1_, ...), custom_call_target="tpu_custom_call" | custom-call | tf_op jit(solution)/shard_map/write_out/pallas_call | solution.py:400

commit v5 on v3

--- a/solution.py
+++ b/solution.py
@@ -76,13 +76,12 @@
     q_hbm, g_hbm, k_hbm, v_hbm, count_hbm, id_hbm, bias_hbm,
     context_out, query_out, key_out, value_out, bias_out,
     q_buf, g_buf, k_buf, v_buf, k_turn, v_turn, counts, ids, line, wide_line, bias_map,
-    s_buf, d_buf, w_all, ds_all, bias_sum, c_buf, dq_buf, dk_buf, dv_buf, parts, bias_row,
+    s_buf, d_buf, w_all, ds_all, bias_sum, c_buf, dq_buf, dk_buf, dv_buf, dp_parts, seq_parts,
     load_sem, own_sem, store_sem,
-    q_send, q_recv, g_send, g_recv, c_send, c_recv, dq_send, dq_recv, b_send, b_recv,
+    q_send, q_recv, g_send, g_recv, c_send, c_recv, dq_send, dq_recv,
+    dp_send, dp_recv, seq_send, seq_recv,
 ):
     dp, seq, enc = lax.axis_index("dp"), lax.axis_index("seq"), lax.axis_index("enc")
-    total = n_dp * n_seq
-    flat = dp * n_seq + seq
     table = line.shape[1]
 
     together = 2 if n_enc % 2 == 0 else 1
@@ -104,22 +103,29 @@
     def from_peer(step):
         return partner(step) if paired else lax.rem(enc + (n_enc - step), n_enc)
 
-    def group_at(place):
-        return (place // n_seq, lax.rem(place, n_seq), enc)
-
-    def other(step):
-        return lax.rem(flat + step, total)
+    def at_dp(place):
+        return (place, seq, enc)
+
+    def at_seq(place):
+        return (dp, place, enc)
 
     barrier = pltpu.get_barrier_semaphore()
 
     def greet(step):
         pl.semaphore_signal(barrier, inc=1, device_id=(dp, seq, to_peer(step)), device_id_type=MESH)
 
-    def greet_group(step):
-        pl.semaphore_signal(barrier, inc=1, device_id=group_at(other(step)), device_id_type=MESH)
-
+    def greet_place(place):
+        pl.semaphore_signal(barrier, inc=1, device_id=place, device_id_type=MESH)
+
+    neighbours = [
+        (dp > 0, at_dp(dp - 1)),
+        (dp < n_dp - 1, at_dp(dp + 1)),
+        (seq > 0, at_seq(seq - 1)),
+        (seq < n_seq - 1, at_seq(seq + 1)),
+    ]
     each(1, n_enc, greet)
-    each(1, total, greet_group)
+    for there, place in neighbours:
+        pl.when(there)(functools.partial(greet_place, place))
 
     loads = [
         (bias_hbm, line),
@@ -133,7 +139,11 @@
     loads = [pltpu.make_async_copy(a, b, load_sem.at[i]) for i, (a, b) in enumerate(loads)]
     for load in loads:
         load.start()
-    pl.semaphore_wait(barrier, n_enc - 1 + total - 1)
+    around = 0
+    for place, size in ((dp, n_dp), (seq, n_seq)):
+        for distance in (place, size - 1 - place):
+            around = around + (distance + size - 1) // size
+    pl.semaphore_wait(barrier, n_enc - 1 + around)
 
     def q_copy(step):
         return pltpu.make_async_remote_copy(
@@ -159,11 +169,55 @@
             dq_send.at[step], dq_recv.at[step], (dp, seq, from_peer(step)), MESH,
         )
 
-    def b_copy(step, place):
-        return pltpu.make_async_remote_copy(
-            bias_row, parts.at[place],
-            b_send.at[step], b_recv.at[step], group_at(other(step)), MESH,
-        )
+    def line_of(place, size, at, parts, send, recv):
+        def hop(side, k):
+            slot = place + k if side == 0 else place - k
+            target = place - 1 if side == 0 else place + 1
+            return pltpu.make_async_remote_copy(
+                parts.at[slot], parts.at[slot],
+                send.at[side * size + k], recv.at[slot], at(target), MESH,
+            )
+
+        def has(side, k):
+            return place + k < size if side == 0 else place >= k
+
+        def onward(side):
+            return place > 0 if side == 0 else place < size - 1
+
+        def arrival(side, k):
+            slot = place + k if side == 0 else place - k
+            origin = place + 1 if side == 0 else place - 1
+            pltpu.make_async_remote_copy(
+                parts.at[slot], parts.at[slot],
+                send.at[side * size + k], recv.at[slot], at(origin), MESH,
+            ).wait_recv()
+
+        def start(row):
+            parts[place] = row
+            for side in (0, 1):
+                pl.when(onward(side))(lambda side=side: hop(side, 0).start())
+
+        def step(k):
+            for side in (0, 1):
+                pl.when(has(side, k))(lambda side=side: arrival(side, k))
+                pl.when(has(side, k) & onward(side))(lambda side=side: hop(side, k).start())
+
+        def end():
+            for k in range(size - 1):
+                for side in (0, 1):
+                    pl.when(has(side, k) & onward(side))(
+                        lambda side=side, k=k: hop(side, k).wait_send()
+                    )
+
+        def added():
+            return functools.reduce(jnp.add, [parts[k] for k in range(size)])
+
+        return start, step, end, added
+
+    dp_start, dp_step, dp_end, dp_added = line_of(dp, n_dp, at_dp, dp_parts, dp_send, dp_recv)
+    seq_start, seq_step, seq_end, seq_added = line_of(
+        seq, n_seq, at_seq, seq_parts, seq_send, seq_recv
+    )
 
     def send_inputs(step):
         q_copy(step).start()
@@ -275,18 +329,17 @@
     for copy in own:
         copy.start()
 
-    def send_bias():
-        bias_row[...] = fold_bias(bias_sum[...])
-        each(1, total, lambda step: b_copy(step, flat).start())
-
     last = groups - 1
     each(1, last, one_batch, unrolled=2)
     if last > 0:
         each_of(last, arrive)
         weigh(last)
-    send_bias()
+    dp_start(fold_bias(bias_sum[...]))
     if last > 0:
         give_back(last)
+    for k in range(1, n_dp):
+        dp_step(k)
+    seq_start(dp_added())
 
     dk_buf[...] = (dot(ds_all[...], q_buf[...], 1, 0) * SCALE).astype(BF16)
     key_store = pltpu.make_async_copy(dk_buf, key_out, store_sem.at[0])
@@ -295,15 +348,9 @@
     value_store = pltpu.make_async_copy(dv_buf, value_out, store_sem.at[1])
     value_store.start()
 
-    parts[flat] = bias_row[...]
-
-    def end_bias(step):
-        b_copy(step, lax.rem(flat + (total - step), total)).wait_recv()
-
-    each(1, total, end_bias)
-    bias_total = parts[0]
-    for place in range(1, total):
-        bias_total = bias_total + parts[place]
+    for k in range(1, n_seq):
+        seq_step(k)
+    bias_total = seq_added()
     line[...] = bias_total[:, 0:table]
     bias_store = pltpu.make_async_copy(line, bias_out, store_sem.at[2])
     bias_store.start()
@@ -317,7 +364,8 @@
         dq_copy(step, to_peer(step)).wait_recv()
 
     each(1, n_enc, end_sends)
-    each(1, total, lambda step: b_copy(step, flat).wait_send())
+    dp_end()
+    seq_end()
     for copy in own:
         copy.wait()
     key_store.wait()
@@ -342,7 +390,6 @@
     tokens = pool * PASSAGE
     slots = neighbour_ids.shape[-1]
     table = rel_bias.shape[1]
-    total = n_dp * n_seq
     all_rows = n_enc * ROWS
     batch_rows = ROWS * (2 if n_enc % 2 == 0 else 1)
     anywhere = pl.BlockSpec(memory_space=pl.ANY)
@@ -379,14 +426,19 @@
             pltpu.VMEM((all_rows, HEAD_DIM), BF16),
             pltpu.VMEM((tokens, HEAD_DIM), BF16),
             pltpu.VMEM((tokens, HEAD_DIM), BF16),
-            pltpu.VMEM((total, 1, WIDE), F32),
-            pltpu.VMEM((1, WIDE), F32),
+            pltpu.VMEM((n_dp, 1, WIDE), F32),
+            pltpu.VMEM((n_seq, 1, WIDE), F32),
             pltpu.SemaphoreType.DMA((7,)),
             pltpu.SemaphoreType.DMA((2,)),
             pltpu.SemaphoreType.DMA((3,)),
         ]
         + [pltpu.SemaphoreType.DMA((n_enc,))] * 8
-        + [pltpu.SemaphoreType.DMA((total,))] * 2,
+        + [
+            pltpu.SemaphoreType.DMA((2 * n_dp,)),
+            pltpu.SemaphoreType.DMA((n_dp,)),
+            pltpu.SemaphoreType.DMA((2 * n_seq,)),
+            pltpu.SemaphoreType.DMA((n_seq,)),
+        ],
         compiler_params=pltpu.CompilerParams(
             collective_id=0, has_side_effects=True, vmem_limit_bytes=48 * 1024 * 1024
         ),

time: 18.1 us -> 23.6 us (1.30)
  Pallas kernels: 17.3 us -> 22.8 us
    pallas_call x1, Pallas kernels: 16.3 us -> 21.9 us  [local(): pl.pallas_call(functools.partial(kernel, n_dp, n_seq, n_enc, pool, slots)...]
where the time goes in v5:
time: 23.6 us; the launch traced here: 23.5 us
  Pallas kernels  22.8 us (97%)
  between operations  0.64 us (3%)
    pallas_call x1, Pallas kernels, local(): pl.pallas_call(functools.partial(kernel, n_dp, n_seq, n_enc, pool, slots)...  21.9 us
    pallas_call x1, Pallas kernels, local(): pl.pallas_call(write_out, out_shape=[jax.ShapeDtypeStruct(x.shape, x.dtyp...  0.92 us

profile of v5, /device:TPU:0, one launch (start us, length us, event | category | flops | bytes accessed | tf_op | source)
XLA Modules:
  0.0 23.5 jit_solution(16577994047576225079)
XLA Ops:
  0.6 21.9 %retrieval_attention.1 = (bf16[1,128,512]{2,1,0:T(8,128)(2,1)S(1)}, bf16[1,128,512]{2,1,0:T(8,128)(2,1)S(1)}, bf16[1024,128]{1,0:T(8,128)(2,1)S(1)}, bf16[1024,128]{1,0:T(8,128)(2,1)S(1)}, f32[1,191]{1,0:T(1,128)S(1)}) custom-call(bf16[1,128,512]{2,1,0:T(8,128)(2,1)} %q_hbm.1, bf16[1,128,512]{2,1,0:T(8,128)(2,1)} %g_hbm.1, bf16[1024,128]{1,0:T(8,128)(2,1)} %bitcast.5, ...), custom_call_target="tpu_custom_call" | custom-call | tf_op jit(solution)/shard_map/retrieval_attention/pallas_call | solution.py:397
  22.5 0.9 %write_out.1 = (bf16[1,128,512]{2,1,0:T(8,128)(2,1)}, bf16[1,128,512]{2,1,0:T(8,128)(2,1)}, bf16[1024,128]{1,0:T(8,128)(2,1)}, bf16[1024,128]{1,0:T(8,128)(2,1)}, f32[1,191]{1,0:T(1,128)}) custom-call(bf16[1,128,512]{2,1,0:T(8,128)(2,1)S(1)} %get-tuple-element.15.refs_0_, bf16[1,128,512]{2,1,0:T(8,128)(2,1)S(1)} %get-tuple-element.16.refs_1_, ...), custom_call_target="tpu_custom_call" | custom-call | tf_op jit(solution)/shard_map/write_out/pallas_call | solution.py:455

commit v6 on v3

--- a/solution.py
+++ b/solution.py
@@ -267,24 +267,26 @@
         weigh(batch)
         give_back(batch)
 
-    one_batch(0)
+    each_of(0, arrive)
+    weigh(0)
+
+    def send_bias():
+        bias_row[...] = fold_bias(bias_sum[...])
+        each(1, total, lambda step: b_copy(step, flat).start())
+
+    last = groups - 1
+    each(1, last, one_batch, unrolled=2)
+    if last > 0:
+        each_of(last, arrive)
+        weigh(last)
+    send_bias()
+    give_back(0)
     own = [
         pltpu.make_async_copy(c_buf.at[span(0)], context_out.at[0, :, span(enc)], own_sem.at[0]),
         pltpu.make_async_copy(dq_buf.at[span(0)], query_out.at[0, :, span(enc)], own_sem.at[1]),
     ]
     for copy in own:
         copy.start()
-
-    def send_bias():
-        bias_row[...] = fold_bias(bias_sum[...])
-        each(1, total, lambda step: b_copy(step, flat).start())
-
-    last = groups - 1
-    each(1, last, one_batch, unrolled=2)
-    if last > 0:
-        each_of(last, arrive)
-        weigh(last)
-    send_bias()
     if last > 0:
         give_back(last)
 

time: 18.1 us -> 18.7 us (1.033)
  Pallas kernels: 17.3 us -> 18 us
    pallas_call x1, Pallas kernels: 16.3 us -> 17 us  [local(): pl.pallas_call(functools.partial(kernel, n_dp, n_seq, n_enc, pool, slots)...]
where the time goes in v6:
time: 18.7 us; the launch traced here: 18.6 us
  Pallas kernels  18 us (96%)
  between operations  0.64 us (3%)
    pallas_call x1, Pallas kernels, local(): pl.pallas_call(functools.partial(kernel, n_dp, n_seq, n_enc, pool, slots)...  17 us
    pallas_call x1, Pallas kernels, local(): pl.pallas_call(write_out, out_shape=[jax.ShapeDtypeStruct(x.shape, x.dtyp...  0.92 us

profile of v6, /device:TPU:0, one launch (start us, length us, event | category | flops | bytes accessed | tf_op | source)
XLA Modules:
  0.0 18.6 jit_solution(13952492089534515627)
XLA Ops:
  0.6 17.0 %retrieval_attention.1 = (bf16[1,128,512]{2,1,0:T(8,128)(2,1)S(1)}, bf16[1,128,512]{2,1,0:T(8,128)(2,1)S(1)}, bf16[1024,128]{1,0:T(8,128)(2,1)S(1)}, bf16[1024,128]{1,0:T(8,128)(2,1)S(1)}, f32[1,191]{1,0:T(1,128)S(1)}) custom-call(bf16[1,128,512]{2,1,0:T(8,128)(2,1)} %q_hbm.1, bf16[1,128,512]{2,1,0:T(8,128)(2,1)} %g_hbm.1, bf16[1024,128]{1,0:T(8,128)(2,1)} %bitcast.5, ...), custom_call_target="tpu_custom_call" | custom-call | tf_op jit(solution)/shard_map/retrieval_attention/pallas_call | solution.py:352
  17.7 0.9 %write_out.1 = (bf16[1,128,512]{2,1,0:T(8,128)(2,1)}, bf16[1,128,512]{2,1,0:T(8,128)(2,1)}, bf16[1024,128]{1,0:T(8,128)(2,1)}, bf16[1024,128]{1,0:T(8,128)(2,1)}, f32[1,191]{1,0:T(1,128)}) custom-call(bf16[1,128,512]{2,1,0:T(8,128)(2,1)S(1)} %get-tuple-element.15.refs_0_, bf16[1,128,512]{2,1,0:T(8,128)(2,1)S(1)} %get-tuple-element.16.refs_1_, ...), custom_call_target="tpu_custom_call" | custom-call | tf_op jit(solution)/shard_map/write_out/pallas_call | solution.py:405

commit v7 on v3

--- a/solution.py
+++ b/solution.py
@@ -171,7 +171,7 @@
 
     each(1, n_enc, lambda step: send_inputs(n_enc - step))
 
-    for load in loads:
+    for load in loads[:3]:
         load.wait()
     wide_line[...] = jnp.zeros_like(wide_line)
     wide_line[:, 0:table] = line[...]
@@ -179,6 +179,8 @@
     for at in range(together):
         bias_map[:, span(at)] = bias_one
     bias_sum[...] = jnp.zeros_like(bias_sum)
+    for load in loads[3:]:
+        load.wait()
     for p in range(pool):
         k_turn[:, p * PASSAGE : (p + 1) * PASSAGE] = k_buf[p * PASSAGE : (p + 1) * PASSAGE, :].T
         v_turn[:, p * PASSAGE : (p + 1) * PASSAGE] = v_buf[p * PASSAGE : (p + 1) * PASSAGE, :].T

time: 18.1 us -> 18.1 us (level)
  no operation moved by 1% of the time
where the time goes in v7:
time: 18.1 us; the launch traced here: 17.9 us
  Pallas kernels  17.3 us (96%)
  between operations  0.64 us (4%)
    pallas_call x1, Pallas kernels, local(): pl.pallas_call(functools.partial(kernel, n_dp, n_seq, n_enc, pool, slots)...  16.3 us
    pallas_call x1, Pallas kernels, local(): pl.pallas_call(write_out, out_shape=[jax.ShapeDtypeStruct(x.shape, x.dtyp...  0.92 us

profile of v7, /device:TPU:0, one launch (start us, length us, event | category | flops | bytes accessed | tf_op | source)
XLA Modules:
  0.0 17.9 jit_solution(12511226835194992473)
XLA Ops:
  0.6 16.3 %retrieval_attention.1 = (bf16[1,128,512]{2,1,0:T(8,128)(2,1)S(1)}, bf16[1,128,512]{2,1,0:T(8,128)(2,1)S(1)}, bf16[1024,128]{1,0:T(8,128)(2,1)S(1)}, bf16[1024,128]{1,0:T(8,128)(2,1)S(1)}, f32[1,191]{1,0:T(1,128)S(1)}) custom-call(bf16[1,128,512]{2,1,0:T(8,128)(2,1)} %q_hbm.1, bf16[1,128,512]{2,1,0:T(8,128)(2,1)} %g_hbm.1, bf16[1024,128]{1,0:T(8,128)(2,1)} %bitcast.5, ...), custom_call_target="tpu_custom_call" | custom-call | tf_op jit(solution)/shard_map/retrieval_attention/pallas_call | solution.py:352
  17.0 0.9 %write_out.1 = (bf16[1,128,512]{2,1,0:T(8,128)(2,1)}, bf16[1,128,512]{2,1,0:T(8,128)(2,1)}, bf16[1024,128]{1,0:T(8,128)(2,1)}, bf16[1024,128]{1,0:T(8,128)(2,1)}, f32[1,191]{1,0:T(1,128)}) custom-call(bf16[1,128,512]{2,1,0:T(8,128)(2,1)S(1)} %get-tuple-element.15.refs_0_, bf16[1,128,512]{2,1,0:T(8,128)(2,1)S(1)} %get-tuple-element.16.refs_1_, ...), custom_call_target="tpu_custom_call" | custom-call | tf_op jit(solution)/shard_map/write_out/pallas_call | solution.py:405
